TPU v7x, 32 devices: a whole 2x2x4 slice. The times are simulated.
32 devices in a mesh: grp: 2 (over y), store: 4 (over z), tp: 4 (over x, core).
Axes of the slice: x: 2, y: 2, z: 4, core: 2. Of those that a mesh axis runs over, the one named last changes fastest.
Arguments:
- hidden: bfloat16 [512, 2, 8192], P(('grp', 'store'), None, 'tp'), parts along dimension 0, may hold values from -6 to 6
- queries: bfloat16 [512, 2, 8192], P(('grp', 'store'), None, 'tp'), parts along dimension 0, may hold values from -16 to 16
- fresh_rotated_keys: bfloat16 [512, 2, 1024], P(('grp', 'store'), None, 'tp'), parts along dimension 0, may hold values from -6 to 6
- value_matrix: bfloat16 [8192, 1024], P('tp'), may hold values from -0.0625 to 0.0625
- adapter_down_factors: bfloat16 [8, 8192, 64], P('store', 'tp'), may hold values from -0.0625 to 0.0625
- adapter_up_factors: bfloat16 [8, 64, 1024], P('store', None, 'tp'), may hold values from -0.375 to 0.375
- adapter_index_rows: int32 [512, 1], P(('grp', 'store')), parts along dimension 0, may hold values from 0 to 7; in each aligned block of 64 rows (0 to 63, 64 to 127, ...) at most 16 rows name the same one
- key_value_pool: bfloat16 [2, 128, 16, 1024], P(None, ('grp', 'store'), None, 'tp'), parts along dimension 1, may hold values from -6 to 6
- row_page_table: int32 [512, 64], P(('grp', 'store')), parts along dimension 0, may hold values from 0 to 15
- context_length: int32 [512], P(('grp', 'store')), parts along dimension 0, may hold values from 1 to 1024
- relocated_rows: int32 [128], P(('grp', 'store')), parts along dimension 0, may hold values from 0 to 63, as said below
- relocated_destination: int32 [128, 1], P(('grp', 'store')), parts along dimension 0, may hold values from 0 to 3; in each aligned block of 16 rows (0 to 15, 16 to 31, ...) at most 8 rows name the same one
Outputs:
- attention: bfloat16 [512, 2, 8192], P(('grp', 'store'), None, 'tp'), parts along dimension 0
- fresh_values: bfloat16 [512, 2, 1024], P(('grp', 'store'), None, 'tp'), parts along dimension 0
There are 2 independent parts, one for each index of `grp`. A program takes and returns all parts, laid end to end along the dimension named above; an argument that names none is the same for every part. Nothing has to cross between parts.
Inputs may be any that keep to these rules, and one draw needn't show every extreme that they name: `adapter_index_rows`: in the rows of one store index no adapter is named by more than 16 rows, a bound that some block reaches. `relocated_destination`: among the 16 entries of one store index at most 8 name the same destination. `relocated_rows`: the 16 entries of one store index name distinct rows of that store index. `row_page_table`: entries index the pool of the row's holder.
All inputs are finite; a program needn't handle non-finite values.
Results may differ from a plain program's by a relative error of at most 0.014.
Values may be sent and summed in bfloat16 or wider, within the bound.
A program may use at most 128 MiB of HBM per device.

v0:
```python
import math

import jax
import jax.numpy as jnp
from jax import lax
from jax.sharding import PartitionSpec as P

HEAD_WIDTH = 128


adapter_scale = 2.0
masked_score = -1e30


def as_sent(shard):

    def short(part):
        return part.astype(jnp.bfloat16) if part.dtype == jnp.float32 else part

    return jax.tree.map(short, shard)


def ranks_within(labels, label_count):
    hits = (labels[:, None] == jnp.arange(label_count, dtype=jnp.int32)[None, :]).astype(jnp.int32)
    return jnp.sum((jnp.cumsum(hits, axis=0) - 1) * hits, axis=1)


def pool_attention(query, table, length, key_value_pool, heads_kv):
    count = query.shape[0]
    step_total = query.shape[1]
    group = query.shape[2] // (heads_kv * HEAD_WIDTH)
    pages, page_len = (key_value_pool.shape[1], key_value_pool.shape[2])
    entries = table.shape[1]
    span = entries * page_len
    pool_keys = key_value_pool[0].reshape(pages * page_len, heads_kv, HEAD_WIDTH)
    page_values = key_value_pool[1].reshape(pages, page_len, heads_kv, HEAD_WIDTH)
    block = math.gcd(count, 16)
    scale = 1.0 / math.sqrt(HEAD_WIDTH)

    def one_block(output_pieces):
        q_blk, t_blk, l_blk = output_pieces
        query_h = q_blk.reshape(block, step_total, heads_kv, group, HEAD_WIDTH)
        whole = (
            jnp.einsum("bikgd,ckd->bikgc", query_h, pool_keys, preferred_element_type=jnp.float32)
            * scale
        )
        whole = whole.reshape(block, step_total, heads_kv, group, pages, page_len)
        picked = jax.vmap(lambda one_score, one_table: one_score[:, :, :, one_table, :])(
            whole, t_blk
        )
        picked = picked.reshape(block, step_total, heads_kv, group, span)
        valid = jnp.arange(span, dtype=jnp.int32)[None, :] < l_blk[:, None]
        picked = jnp.where(valid[:, None, None, None, :], picked, masked_score)
        largest = jnp.max(picked, axis=-1)
        expo = jnp.exp(picked - largest[..., None])
        total = jnp.sum(expo, axis=-1)
        weights = expo.astype(jnp.bfloat16)
        row_values = page_values[t_blk].reshape(block, span, heads_kv, HEAD_WIDTH)
        mixed = jnp.einsum(
            "bikgc,bckd->bikgd", weights, row_values, preferred_element_type=jnp.float32
        )
        return (
            mixed.reshape(block, step_total, heads_kv * group * HEAD_WIDTH),
            largest.reshape(block, step_total, heads_kv * group),
            total.reshape(block, step_total, heads_kv * group),
        )

    result = lax.map(
        one_block,
        (
            query.reshape(count // block, block, step_total, -1),
            table.reshape(count // block, block, entries),
            length.reshape(count // block, block),
        ),
    )
    return tuple((piece.reshape((count,) + piece.shape[2:]) for piece in result))


def per_device(
    hidden,
    queries,
    fresh_rotated_keys,
    value_matrix,
    adapter_down_factors,
    adapter_up_factors,
    adapter_index_rows,
    key_value_pool,
    row_page_table,
    context_length,
    relocated_rows,
    relocated_destination,
):
    stores = lax.axis_size("store")
    row_total, step_total, feat_count = hidden.shape
    local_width = fresh_rotated_keys.shape[2]
    heads_kv = local_width // HEAD_WIDTH
    q_width = queries.shape[2]
    group = q_width // local_width
    resident_adapters = adapter_down_factors.shape[0]
    adapter_count = resident_adapters * stores
    most_rows = 2 * row_total // adapter_count
    token_inputs = hidden.reshape(row_total * step_total, feat_count)
    base_part = jnp.dot(token_inputs, value_matrix, preferred_element_type=jnp.float32)
    adapter_of = adapter_index_rows[:, 0]
    slot_index = adapter_of * most_rows + ranks_within(adapter_of, adapter_count)
    outgoing = jnp.zeros((adapter_count * most_rows, step_total, feat_count), jnp.bfloat16)
    outgoing = (
        outgoing.at[slot_index]
        .set(hidden)
        .reshape(stores, resident_adapters * most_rows, step_total, feat_count)
    )
    migrants = relocated_rows.shape[0]
    capacity = max(2, 2 * migrants // stores)
    dest_of = relocated_destination[:, 0]
    moved_slot = dest_of * capacity + ranks_within(dest_of, stores)
    moved_q = jnp.zeros((stores * capacity, step_total, q_width), jnp.bfloat16)
    moved_q = (
        moved_q.at[moved_slot]
        .set(queries[relocated_rows])
        .reshape(stores, capacity, step_total, q_width)
    )
    moved_t = jnp.zeros((stores * capacity, row_page_table.shape[1]), jnp.int32)
    moved_t = (
        moved_t.at[moved_slot]
        .set(row_page_table[relocated_rows])
        .reshape(stores, capacity, row_page_table.shape[1])
    )
    moved_l = jnp.zeros((stores * capacity,), jnp.int32)
    moved_l = moved_l.at[moved_slot].set(context_length[relocated_rows]).reshape(stores, capacity)
    arrived = lax.all_to_all(outgoing, "store", split_axis=0, concat_axis=0, tiled=True)
    got_q, got_t, got_l = (
        lax.all_to_all(moved_q, "store", split_axis=0, concat_axis=0, tiled=True),
        lax.all_to_all(moved_t, "store", split_axis=0, concat_axis=0, tiled=True),
        lax.all_to_all(moved_l, "store", split_axis=0, concat_axis=0, tiled=True),
    )
    far_o, far_m, far_l = pool_attention(
        got_q.reshape(stores * capacity, step_total, q_width),
        got_t.reshape(stores * capacity, -1),
        got_l.reshape(stores * capacity),
        key_value_pool,
        heads_kv,
    )
    back_o, back_m, back_l = (
        lax.all_to_all(
            far_o.reshape(stores, capacity, step_total, -1).astype(jnp.bfloat16),
            "store",
            split_axis=0,
            concat_axis=0,
            tiled=True,
        ).astype(jnp.float32),
        lax.all_to_all(
            as_sent(far_m.reshape(stores, capacity, step_total, -1)),
            "store",
            split_axis=0,
            concat_axis=0,
            tiled=True,
        ),
        lax.all_to_all(
            as_sent(far_l.reshape(stores, capacity, step_total, -1)),
            "store",
            split_axis=0,
            concat_axis=0,
            tiled=True,
        ),
    )
    moved_mask = jnp.zeros((row_total,), jnp.int32).at[relocated_rows].set(1)
    staying = jnp.argsort(moved_mask, stable=True)[: row_total - migrants]
    near_o, near_m, near_l = pool_attention(
        queries[staying], row_page_table[staying], context_length[staying], key_value_pool, heads_kv
    )
    block_tiles = arrived.reshape(stores, resident_adapters, most_rows * step_total, feat_count)
    block_tiles = block_tiles.transpose(1, 0, 2, 3).reshape(
        resident_adapters, stores * most_rows * step_total, feat_count
    )
    partial_middle = jnp.einsum(
        "mks,msb->mkb", block_tiles, adapter_down_factors, preferred_element_type=jnp.float32
    )
    middle_sum = lax.psum(partial_middle.astype(jnp.bfloat16), "tp").astype(jnp.float32)
    term = jnp.einsum(
        "ejb,eby->ejy",
        middle_sum,
        adapter_up_factors.astype(jnp.float32),
        precision=lax.Precision.HIGHEST,
    )
    values = term
    width = values.shape[2]
    values = values.reshape(resident_adapters, stores, most_rows, step_total, width)
    returned = lax.all_to_all(
        values.transpose(1, 0, 2, 3, 4)
        .reshape(stores, resident_adapters * most_rows, step_total, width)
        .astype(jnp.bfloat16),
        "store",
        split_axis=0,
        concat_axis=0,
        tiled=True,
    ).astype(jnp.float32)
    row_summand = returned.reshape(adapter_count * most_rows, step_total, local_width)[slot_index]
    extra_output = adapter_scale * row_summand.reshape(row_total * step_total, local_width)
    value_sum = (
        lax.psum_scatter(
            base_part.astype(jnp.bfloat16), "tp", scatter_dimension=1, tiled=True
        ).astype(jnp.float32)
        + extra_output
    )
    fresh_values = value_sum.astype(jnp.bfloat16).reshape(row_total, step_total, local_width)
    flat_back_o = back_o.reshape(stores * capacity, step_total, -1)[moved_slot]
    flat_back_m = back_m.reshape(stores * capacity, step_total, -1)[moved_slot]
    flat_back_l = back_l.reshape(stores * capacity, step_total, -1)[moved_slot]
    cache_o = (
        jnp.zeros((row_total, step_total, q_width), jnp.float32)
        .at[staying]
        .set(near_o)
        .at[relocated_rows]
        .set(flat_back_o)
    )
    cache_m = (
        jnp.zeros((row_total, step_total, q_width // HEAD_WIDTH), jnp.float32)
        .at[staying]
        .set(near_m)
        .at[relocated_rows]
        .set(flat_back_m)
    )
    cache_l = (
        jnp.zeros((row_total, step_total, q_width // HEAD_WIDTH), jnp.float32)
        .at[staying]
        .set(near_l)
        .at[relocated_rows]
        .set(flat_back_l)
    )
    scale = 1.0 / math.sqrt(HEAD_WIDTH)
    query_h = queries.reshape(row_total, step_total, heads_kv, group, HEAD_WIDTH)
    key_new = fresh_rotated_keys.reshape(row_total, step_total, heads_kv, HEAD_WIDTH)
    value_new = fresh_values.reshape(row_total, step_total, heads_kv, HEAD_WIDTH)
    s_new = (
        jnp.einsum("bikgd,bjkd->bikgj", query_h, key_new, preferred_element_type=jnp.float32)
        * scale
    )
    causal = jnp.arange(step_total)[None, :] <= jnp.arange(step_total)[:, None]
    s_new = jnp.where(causal[None, :, None, None, :], s_new, masked_score)
    cache_top = cache_m.reshape(row_total, step_total, heads_kv, group)
    largest = jnp.maximum(cache_top, jnp.max(s_new, axis=-1))
    keep = jnp.exp(cache_top - largest)
    expo = jnp.exp(s_new - largest[..., None])
    total = cache_l.reshape(row_total, step_total, heads_kv, group) * keep + jnp.sum(expo, axis=-1)
    mixed = cache_o.reshape(row_total, step_total, heads_kv, group, HEAD_WIDTH) * keep[..., None]
    mixed = mixed + jnp.einsum(
        "bikgj,bjkd->bikgd",
        expo.astype(jnp.bfloat16),
        value_new,
        preferred_element_type=jnp.float32,
    )
    attention = (
        (mixed / total[..., None]).reshape(row_total, step_total, q_width).astype(jnp.bfloat16)
    )
    return (attention, fresh_values)


def solution(mesh):
    placed = (
        P(("grp", "store"), None, "tp"),
        P(("grp", "store"), None, "tp"),
        P(("grp", "store"), None, "tp"),
        P("tp", None),
        P("store", "tp", None),
        P("store", None, "tp"),
        P(("grp", "store"), None),
        P(None, ("grp", "store"), None, "tp"),
        P(("grp", "store"), None),
        P(("grp", "store")),
        P(("grp", "store")),
        P(("grp", "store"), None),
    )
    return jax.shard_map(
        per_device,
        mesh=mesh,
        in_specs=placed,
        out_specs=(P(("grp", "store"), None, "tp"), P(("grp", "store"), None, "tp")),
        check_vma=False,
    )
```

profile of v0, /device:TPU:0, one launch (start us, length us, event | category | flops | bytes accessed | tf_op | source)
XLA Modules:
  0.0 816.3 jit_solution(7144533855274998371)
XLA Ops:
  12.8 6.3 all-to-all-start.1
  26.1 5.1 all-to-all-start
  49.2 279.8 %while.29 = (s32[]{:T(128)}, bf16[2,16,2,2048]{3,1,0,2:T(8,128)(2,1)}, bf16[2,16,2,16]{3,1,0,2:T(8,128)(2,1)S(1)}, bf16[2,16,2,16]{3,1,0,2:T(8,128)(2,1)S(1)}, s...) while((s32[]{:T(128)}, ...), condition=%wide.region_15.16_spmd, body=%wide.region_12.15_spmd.sunk | while | flops 172140544 | bytes 48554868 | solution.py:68
  74.1 6.1 copy.393
  80.2 16.1 %gather_fusion.3 = f32[1024,2,2,8,16]{4,3,2,1,0:T(8,128)} fusion(f32[16,2,2,8,16,16]{5,3,4,2,1,0:T(8,128)} %copy.393, s32[1024]{0:T(1024)S(1)} %reshape.600), kind=kCustom, calls=%fused_computation.3.clone.1 | custom fusion | bytes 4202496 | tf_op jit(solution)/shard_map/while/body/eval_jaxpr/vmap()/gather | solution.py:48
  96.5 21.3 %select_reduce_fusion.7 = f32[16,2,2,8]{3,2,1,0:T(2,128)S(1)} fusion(pred[16,64,16]{2,1,0:T(8,128)(4,1)S(1)} %broadcast_compare_fusion.5, f32[16,64,2,2,8,16]{5,4,3,2,1,0:T(8,128)} %bitcast.239), kind=kLoop, calls=%fused_computation.51.clone.1 | loop fusion | flops 1048064 | bytes 2115584 | tf_op jit(solution)/shard_map/while/body/eval_jaxpr/reduce_max | solution.py:54
  117.7 19.0 %exponential_reduce_fusion.5 = bf16[16,2,2,8]{3,2,1,0:T(2,128)(2,1)S(1)} fusion(f32[16,2,2,8]{3,2,1,0:T(2,128)S(1)} %select_reduce_fusion.7, pred[16,64,16]{2,1,0:T(8,128)(4,1)S(1)} %broadcast_compare_fusion.5, f32[16,64,2,2,8,16]{5,4,3,2,1,0:T(8,128)} %bitcast.240), kind=kLoop, calls=%fused_computation.50.clone.1 | loop fusion | flops 1572352 | bytes 2116608 | tf_op jit(solution)/shard_map/while/body/eval_jaxpr/reduce_sum | solution.py:56
  137.1 17.7 %copy.394 = f32[16,64,2,2,8,16]{5,1,4,3,2,0:T(8,128)} copy(f32[16,64,2,2,8,16]{5,4,3,2,1,0:T(8,128)} %bitcast.241) | data formatting | bytes 4194304 | tf_op jit(solution)/shard_map/while/body/eval_jaxpr/vmap()/gather | solution.py:48
  154.8 14.2 %reshape.601 = f32[16,2,2,8,1024]{4,3,2,1,0:T(8,128)S(1)} reshape(f32[16,2,2,8,64,16]{5,4,3,2,1,0:T(8,128)} %bitcast.245) | data formatting | bytes 4194304 | tf_op jit(solution)/shard_map/while/body/eval_jaxpr/reshape | solution.py:51
  169.0 25.2 %gather_fusion.2 = bf16[1024,16,2,128]{3,2,1,0:T(2,128)(2,1)} fusion(bf16[16,16,2,128]{3,2,1,0:T(2,128)(2,1)S(1)} %get-tuple-element.439, s32[1024]{0:T(1024)S(1)} %broadcast_clamp_fusion.5), kind=kCustom, calls=%fused_computation.2.clone.1 | custom fusion | bytes 16781312 | tf_op jit(solution)/shard_map/while/body/eval_jaxpr/gather | solution.py:58
  194.3 4.8 fusion.81
  202.8 6.1 copy.393
  208.9 16.1 %gather_fusion.3 = f32[1024,2,2,8,16]{4,3,2,1,0:T(8,128)} fusion(f32[16,2,2,8,16,16]{5,3,4,2,1,0:T(8,128)} %copy.393, s32[1024]{0:T(1024)S(1)} %reshape.600), kind=kCustom, calls=%fused_computation.3.clone.1 | custom fusion | bytes 4202496 | tf_op jit(solution)/shard_map/while/body/eval_jaxpr/vmap()/gather | solution.py:48
  225.2 21.3 %select_reduce_fusion.7 = f32[16,2,2,8]{3,2,1,0:T(2,128)S(1)} fusion(pred[16,64,16]{2,1,0:T(8,128)(4,1)S(1)} %broadcast_compare_fusion.5, f32[16,64,2,2,8,16]{5,4,3,2,1,0:T(8,128)} %bitcast.239), kind=kLoop, calls=%fused_computation.51.clone.1 | loop fusion | flops 1048064 | bytes 2115584 | tf_op jit(solution)/shard_map/while/body/eval_jaxpr/reduce_max | solution.py:54
  246.4 19.0 %exponential_reduce_fusion.5 = bf16[16,2,2,8]{3,2,1,0:T(2,128)(2,1)S(1)} fusion(f32[16,2,2,8]{3,2,1,0:T(2,128)S(1)} %select_reduce_fusion.7, pred[16,64,16]{2,1,0:T(8,128)(4,1)S(1)} %broadcast_compare_fusion.5, f32[16,64,2,2,8,16]{5,4,3,2,1,0:T(8,128)} %bitcast.240), kind=kLoop, calls=%fused_computation.50.clone.1 | loop fusion | flops 1572352 | bytes 2116608 | tf_op jit(solution)/shard_map/while/body/eval_jaxpr/reduce_sum | solution.py:56
  265.8 17.7 %copy.394 = f32[16,64,2,2,8,16]{5,1,4,3,2,0:T(8,128)} copy(f32[16,64,2,2,8,16]{5,4,3,2,1,0:T(8,128)} %bitcast.241) | data formatting | bytes 4194304 | tf_op jit(solution)/shard_map/while/body/eval_jaxpr/vmap()/gather | solution.py:48
  283.5 14.2 %reshape.601 = f32[16,2,2,8,1024]{4,3,2,1,0:T(8,128)S(1)} reshape(f32[16,2,2,8,64,16]{5,4,3,2,1,0:T(8,128)} %bitcast.245) | data formatting | bytes 4194304 | tf_op jit(solution)/shard_map/while/body/eval_jaxpr/reshape | solution.py:51
  297.7 25.2 %gather_fusion.2 = bf16[1024,16,2,128]{3,2,1,0:T(2,128)(2,1)} fusion(bf16[16,16,2,128]{3,2,1,0:T(2,128)(2,1)S(1)} %get-tuple-element.439, s32[1024]{0:T(1024)S(1)} %broadcast_clamp_fusion.5), kind=kCustom, calls=%fused_computation.2.clone.1 | custom fusion | bytes 16781312 | tf_op jit(solution)/shard_map/while/body/eval_jaxpr/gather | solution.py:58
  323.0 4.8 fusion.81
  347.3 8.8 %scatter_fusion.5 = bf16[128,2,2048]{2,1,0:T(2,128)(2,1)} fusion(bf16[128,2,2048]{2,1,0:T(2,128)(2,1)} %broadcast_in_dim.138, s32[64]{0:T(128)S(1)} %copy-done.16, bf16[64,2,2048]{2,1,0:T(2,128)(2,1)} %param.16), kind=kCustom, calls=%fused_computation.22 | custom fusion | bytes 1573120 | tf_op jit(solution)/shard_map/scatter | solution.py:109
  356.1 5.0 all-to-all-start.5
  361.2 395.1 %while.28 = (s32[]{:T(128)}, f32[3,16,2,2048]{3,1,0,2:T(8,128)}, f32[3,16,2,16]{3,2,1,0:T(2,128)S(1)}, f32[3,16,2,16]{3,2,1,0:T(2,128)S(1)}, s32[3,16,64]{2,1,0:...) while((s32[]{:T(128)}, f32[3,16,2,2048]{3,1,0,2:T(8,128)}, ...), condition=%wide.region_5.6_spmd, body=%wide.region_2.0_spmd.sunk | while | flops 172140544 | bytes 49513332 | solution.py:68
  364.5 6.1 copy.380
  370.6 16.1 %gather_fusion.1 = f32[1024,2,2,8,16]{4,3,2,1,0:T(8,128)} fusion(f32[16,2,2,8,16,16]{5,3,4,2,1,0:T(8,128)} %copy.380, s32[1024]{0:T(1024)S(1)} %reshape.592), kind=kCustom, calls=%fused_computation.1.clone.1 | custom fusion | bytes 4202496 | tf_op jit(solution)/shard_map/while/body/eval_jaxpr/vmap()/gather | solution.py:48
  386.9 21.3 %select_reduce_fusion.6 = f32[16,2,2,8]{3,2,1,0:T(2,128)S(1)} fusion(pred[16,64,16]{2,1,0:T(8,128)(4,1)S(1)} %broadcast_compare_fusion.4, f32[16,64,2,2,8,16]{5,4,3,2,1,0:T(8,128)} %bitcast.242), kind=kLoop, calls=%fused_computation.27.clone.1 | loop fusion | flops 1048064 | bytes 2115584 | tf_op jit(solution)/shard_map/while/body/eval_jaxpr/reduce_max | solution.py:54
  408.1 19.0 %exponential_reduce_fusion.4 = f32[16,2,2,8]{3,2,1,0:T(2,128)S(1)} fusion(f32[16,2,2,8]{3,2,1,0:T(2,128)S(1)} %select_reduce_fusion.6, pred[16,64,16]{2,1,0:T(8,128)(4,1)S(1)} %broadcast_compare_fusion.4, f32[16,64,2,2,8,16]{5,4,3,2,1,0:T(8,128)} %bitcast.243), kind=kLoop, calls=%fused_computation.26.clone.1 | loop fusion | flops 1572352 | bytes 2117632 | tf_op jit(solution)/shard_map/while/body/eval_jaxpr/reduce_sum | solution.py:56
  427.5 17.7 %copy.381 = f32[16,64,2,2,8,16]{5,1,4,3,2,0:T(8,128)} copy(f32[16,64,2,2,8,16]{5,4,3,2,1,0:T(8,128)} %bitcast.244) | data formatting | bytes 4194304 | tf_op jit(solution)/shard_map/while/body/eval_jaxpr/vmap()/gather | solution.py:48
  445.2 14.2 %reshape.593 = f32[16,2,2,8,1024]{4,3,2,1,0:T(8,128)S(1)} reshape(f32[16,2,2,8,64,16]{5,4,3,2,1,0:T(8,128)} %bitcast.246) | data formatting | bytes 4194304 | tf_op jit(solution)/shard_map/while/body/eval_jaxpr/reshape | solution.py:51
  459.4 25.2 %gather_fusion = bf16[1024,16,2,128]{3,2,1,0:T(2,128)(2,1)} fusion(bf16[16,16,2,128]{3,2,1,0:T(2,128)(2,1)S(1)} %get-tuple-element.409, s32[1024]{0:T(1024)S(1)} %broadcast_clamp_fusion.4), kind=kCustom, calls=%fused_computation.clone.1 | custom fusion | bytes 16781312 | tf_op jit(solution)/shard_map/while/body/eval_jaxpr/gather | solution.py:58
  484.6 4.8 fusion.74
  493.3 6.1 copy.380
  499.4 16.1 %gather_fusion.1 = f32[1024,2,2,8,16]{4,3,2,1,0:T(8,128)} fusion(f32[16,2,2,8,16,16]{5,3,4,2,1,0:T(8,128)} %copy.380, s32[1024]{0:T(1024)S(1)} %reshape.592), kind=kCustom, calls=%fused_computation.1.clone.1 | custom fusion | bytes 4202496 | tf_op jit(solution)/shard_map/while/body/eval_jaxpr/vmap()/gather | solution.py:48
  515.7 21.3 %select_reduce_fusion.6 = f32[16,2,2,8]{3,2,1,0:T(2,128)S(1)} fusion(pred[16,64,16]{2,1,0:T(8,128)(4,1)S(1)} %broadcast_compare_fusion.4, f32[16,64,2,2,8,16]{5,4,3,2,1,0:T(8,128)} %bitcast.242), kind=kLoop, calls=%fused_computation.27.clone.1 | loop fusion | flops 1048064 | bytes 2115584 | tf_op jit(solution)/shard_map/while/body/eval_jaxpr/reduce_max | solution.py:54
  537.0 19.0 %exponential_reduce_fusion.4 = f32[16,2,2,8]{3,2,1,0:T(2,128)S(1)} fusion(f32[16,2,2,8]{3,2,1,0:T(2,128)S(1)} %select_reduce_fusion.6, pred[16,64,16]{2,1,0:T(8,128)(4,1)S(1)} %broadcast_compare_fusion.4, f32[16,64,2,2,8,16]{5,4,3,2,1,0:T(8,128)} %bitcast.243), kind=kLoop, calls=%fused_computation.26.clone.1 | loop fusion | flops 1572352 | bytes 2117632 | tf_op jit(solution)/shard_map/while/body/eval_jaxpr/reduce_sum | solution.py:56
  556.3 17.7 %copy.381 = f32[16,64,2,2,8,16]{5,1,4,3,2,0:T(8,128)} copy(f32[16,64,2,2,8,16]{5,4,3,2,1,0:T(8,128)} %bitcast.244) | data formatting | bytes 4194304 | tf_op jit(solution)/shard_map/while/body/eval_jaxpr/vmap()/gather | solution.py:48
  574.0 14.2 %reshape.593 = f32[16,2,2,8,1024]{4,3,2,1,0:T(8,128)S(1)} reshape(f32[16,2,2,8,64,16]{5,4,3,2,1,0:T(8,128)} %bitcast.246) | data formatting | bytes 4194304 | tf_op jit(solution)/shard_map/while/body/eval_jaxpr/reshape | solution.py:51
  588.2 25.2 %gather_fusion = bf16[1024,16,2,128]{3,2,1,0:T(2,128)(2,1)} fusion(bf16[16,16,2,128]{3,2,1,0:T(2,128)(2,1)S(1)} %get-tuple-element.409, s32[1024]{0:T(1024)S(1)} %broadcast_clamp_fusion.4), kind=kCustom, calls=%fused_computation.clone.1 | custom fusion | bytes 16781312 | tf_op jit(solution)/shard_map/while/body/eval_jaxpr/gather | solution.py:58
  613.5 4.8 fusion.74
  622.1 6.1 copy.380
  628.3 16.1 %gather_fusion.1 = f32[1024,2,2,8,16]{4,3,2,1,0:T(8,128)} fusion(f32[16,2,2,8,16,16]{5,3,4,2,1,0:T(8,128)} %copy.380, s32[1024]{0:T(1024)S(1)} %reshape.592), kind=kCustom, calls=%fused_computation.1.clone.1 | custom fusion | bytes 4202496 | tf_op jit(solution)/shard_map/while/body/eval_jaxpr/vmap()/gather | solution.py:48
  644.5 21.3 %select_reduce_fusion.6 = f32[16,2,2,8]{3,2,1,0:T(2,128)S(1)} fusion(pred[16,64,16]{2,1,0:T(8,128)(4,1)S(1)} %broadcast_compare_fusion.4, f32[16,64,2,2,8,16]{5,4,3,2,1,0:T(8,128)} %bitcast.242), kind=kLoop, calls=%fused_computation.27.clone.1 | loop fusion | flops 1048064 | bytes 2115584 | tf_op jit(solution)/shard_map/while/body/eval_jaxpr/reduce_max | solution.py:54
  665.8 19.0 %exponential_reduce_fusion.4 = f32[16,2,2,8]{3,2,1,0:T(2,128)S(1)} fusion(f32[16,2,2,8]{3,2,1,0:T(2,128)S(1)} %select_reduce_fusion.6, pred[16,64,16]{2,1,0:T(8,128)(4,1)S(1)} %broadcast_compare_fusion.4, f32[16,64,2,2,8,16]{5,4,3,2,1,0:T(8,128)} %bitcast.243), kind=kLoop, calls=%fused_computation.26.clone.1 | loop fusion | flops 1572352 | bytes 2117632 | tf_op jit(solution)/shard_map/while/body/eval_jaxpr/reduce_sum | solution.py:56
  685.1 17.7 %copy.381 = f32[16,64,2,2,8,16]{5,1,4,3,2,0:T(8,128)} copy(f32[16,64,2,2,8,16]{5,4,3,2,1,0:T(8,128)} %bitcast.244) | data formatting | bytes 4194304 | tf_op jit(solution)/shard_map/while/body/eval_jaxpr/vmap()/gather | solution.py:48
  702.8 14.2 %reshape.593 = f32[16,2,2,8,1024]{4,3,2,1,0:T(8,128)S(1)} reshape(f32[16,2,2,8,64,16]{5,4,3,2,1,0:T(8,128)} %bitcast.246) | data formatting | bytes 4194304 | tf_op jit(solution)/shard_map/while/body/eval_jaxpr/reshape | solution.py:51
  717.0 25.2 %gather_fusion = bf16[1024,16,2,128]{3,2,1,0:T(2,128)(2,1)} fusion(bf16[16,16,2,128]{3,2,1,0:T(2,128)(2,1)S(1)} %get-tuple-element.409, s32[1024]{0:T(1024)S(1)} %broadcast_clamp_fusion.4), kind=kCustom, calls=%fused_computation.clone.1 | custom fusion | bytes 16781312 | tf_op jit(solution)/shard_map/while/body/eval_jaxpr/gather | solution.py:58
  773.8 5.1 all-to-all-start.3
  782.0 10.6 %psum.7 = bf16[2,128,64]{1,2,0:T(8,128)(2,1)S(1)} all-reduce(bf16[2,128,64]{1,2,0:T(8,128)(2,1)S(1)} %convolution_convert_fusion.2), channel_id=1, replica_groups=mesh['grp'=2,'store'=4,'tp'=4] {'tp'}, use_global_device_ids=true, to_apply=%region_24.25 | all-reduce | flops 16384 | bytes 65536 | tf_op jit(solution)/shard_map/psum | solution.py:178
  793.5 4.8 all-to-all-start.6
  (262 shorter events, 107.9 us)
Async XLA Ops:
  7.2 774.3 %copy-start = (bf16[2,2048,64]{1,2,0:T(8,128)(2,1)S(1)}, bf16[2,2048,64]{1,2,0:T(8,128)(2,1)}, u32[]{:S(2)}) copy-start(bf16[2,2048,64]{1,2,0:T(8,128)(2,1)} %param.20) | copy-start | bytes 1572868
  7.2 34.0 %copy-start.13 = (s32[64,1]{0,1:T(1,128)S(1)}, s32[64,1]{0,1:T(1,128)}, u32[]{:S(2)}) copy-start(s32[64,1]{0,1:T(1,128)} %param.22) | copy-start | bytes 772
  7.9 38.3 %copy-start.11 = (s32[16]{0:T(128)}, s32[16]{0:T(128)S(1)}, u32[]{:S(2)}) copy-start(s32[16]{0:T(128)S(1)} %compare_select_fusion.5) | copy-start | bytes 196
  10.2 30.9 %copy-start.14 = (s32[16]{0:T(128)}, s32[16]{0:T(128)S(1)}, u32[]{:S(2)}) copy-start(s32[16]{0:T(128)S(1)} %fusion.39) | copy-start | bytes 196
  12.8 13.3 %all-to-all-start.1 = ((s32[4,1,8]{2,1,0:T(1,128)}), s32[4,1,8]{2,1,0:T(1,128)S(1)}, u32[]{:S(2)}, u32[]{:S(2)}) async-start(s32[4,1,8]{2,1,0:T(1,128)} %bitcast.32), calls=%async_computation.1 | async-start | bytes 4096 | tf_op jit(solution)/shard_map/all_to_all | solution.py:134
  19.1 786.5 %reduce-scatter.2.cloned.1.call-start = ((), (), s32[]{:S(2)}) async-start(), calls=%async_computation.9 | async-start | bytes 327680 | tf_op jit(solution)/shard_map/reduce_scatter | solution.py:200
  26.1 10.7 %all-to-all-start = ((s32[4,1,512]{2,1,0:T(1,128)}), s32[4,1,512]{2,1,0:T(1,128)S(1)}, u32[]{:S(2)}, u32[]{:S(2)}) async-start(s32[4,1,512]{2,1,0:T(1,128)} %reshape.562), calls=%async_computation | async-start | bytes 16384 | tf_op jit(solution)/shard_map/all_to_all | solution.py:133
  36.8 12.3 %all-to-all-start.2 = ((bf16[4,8,2,2048]{3,1,2,0:T(8,128)(2,1)}), bf16[4,8,2,2048]{3,1,2,0:T(8,128)(2,1)S(1)}, u32[]{:S(2)}, u32[]{:S(2)}) async-start(bf16[4,8,2,2048]{3,1,2,0:T(8,128)(2,1)} %copy.233), calls=%async_computation.2 | async-start | bytes 524288 | tf_op jit(solution)/shard_map/all_to_all | solution.py:132
  49.1 284.0 %copy-start.19 = (s32[64]{0:T(128)S(1)}, s32[64]{0:T(128)}, u32[]{:S(2)}) copy-start(s32[64]{0:T(128)} %get-tuple-element.101) | copy-start | bytes 772
  49.1 295.1 %copy-start.2 = (s32[64,64]{1,0:T(8,128)S(1)}, s32[64,64]{1,0:T(8,128)}, u32[]{:S(2)}) copy-start(s32[64,64]{1,0:T(8,128)} %param.24) | copy-start | bytes 49156
  49.1 295.7 %copy-start.1 = (s32[64]{0:T(128)S(1)}, s32[64]{0:T(128)}, u32[]{:S(2)}) copy-start(s32[64]{0:T(128)} %param.25) | copy-start | bytes 772
  49.2 298.1 %copy-start.16 = (s32[64]{0:T(128)S(1)}, s32[64]{0:T(128)}, u32[]{:S(2)}) copy-start(s32[64]{0:T(128)} %fusion.40) | copy-start | bytes 772
  329.7 8.9 %all-to-all-start.4 = ((bf16[4,2,128]{2,1,0:T(2,128)(2,1)}), bf16[4,2,128]{2,1,0:T(2,128)(2,1)S(1)}, u32[]{:S(2)}, u32[]{:S(2)}) async-start(bf16[4,2,128]{2,1,0:T(2,128)(2,1)} %reshape.564), calls=%async_computation.4 | async-start | bytes 4096 | tf_op jit(solution)/shard_map/all_to_all | solution.py:151
  333.1 8.7 %copy-start.5 = (s32[48]{0:T(128)}, s32[48]{0:T(128)S(1)}, u32[]{:S(2)}) copy-start(s32[48]{0:T(128)S(1)} %compare_select_fusion.4) | copy-start | bytes 580
  338.6 3.3 copy-start.9
  338.6 17.6 %all-to-all-start.7 = ((bf16[4,2,128]{2,1,0:T(2,128)(2,1)}), bf16[4,2,128]{2,1,0:T(2,128)(2,1)S(1)}, u32[]{:S(2)}, u32[]{:S(2)}) async-start(bf16[4,2,128]{2,1,0:T(2,128)(2,1)} %reshape.566), calls=%async_computation.8 | async-start | bytes 4096 | tf_op jit(solution)/shard_map/all_to_all | solution.py:158
  356.1 5.1 copy-start.7
  356.1 417.6 %all-to-all-start.5 = ((bf16[4,32,2,2048]{3,2,1,0:T(2,128)(2,1)}), bf16[4,32,2,2048]{3,2,1,0:T(2,128)(2,1)}, u32[]{:S(2)}, u32[]{:S(2)}) async-start(bf16[4,32,2,2048]{3,2,1,0:T(2,128)(2,1)} %bitcast.48), calls=%async_computation.6 | async-start | bytes 2097152 | tf_op jit(solution)/shard_map/all_to_all | solution.py:130
  361.2 396.6 %copy-start.18 = (bf16[64,2,256]{2,1,0:T(2,128)(2,1)S(1)}, bf16[64,2,256]{2,1,0:T(2,128)(2,1)}, u32[]{:S(2)}) copy-start(bf16[64,2,256]{2,1,0:T(2,128)(2,1)} %param.18) | copy-start | bytes 196612
  361.2 401.0 %copy-start.6 = (s32[48]{0:T(128)S(1)}, s32[48]{0:T(128)}, u32[]{:S(2)}) copy-start(s32[48]{0:T(128)} %copy-done.5) | copy-start | bytes 580
  361.2 407.4 %copy-start.15 = (s32[16]{0:T(128)S(1)}, s32[16]{0:T(128)}, u32[]{:S(2)}) copy-start(s32[16]{0:T(128)} %copy-done.14) | copy-start | bytes 196
  361.2 407.5 %copy-start.17 = (s32[64]{0:T(128)S(1)}, s32[64]{0:T(128)}, u32[]{:S(2)}) copy-start(s32[64]{0:T(128)} %fusion.40) | copy-start | bytes 772
  756.3 12.4 %copy-start.3 = (bf16[2,16,2,2048]{3,1,0,2:T(8,128)(2,1)S(1)}, bf16[2,16,2,2048]{3,1,0,2:T(8,128)(2,1)}, u32[]{:S(2)}) copy-start(bf16[2,16,2,2048]{3,1,0,2:T(8,128)(2,1)} %get-tuple-element.103) | copy-start | bytes 786436
  756.3 13.1 %copy-start.10 = (bf16[4,2,128]{2,1,0:T(2,128)(2,1)S(1)}, bf16[4,2,128]{2,1,0:T(2,128)(2,1)}, u32[]{:S(2)}) copy-start(bf16[4,2,128]{2,1,0:T(2,128)(2,1)} %copy-done.9) | copy-start | bytes 6148
  756.3 13.8 %copy-start.12 = (s32[16]{0:T(128)S(1)}, s32[16]{0:T(128)}, u32[]{:S(2)}) copy-start(s32[16]{0:T(128)} %copy-done.11) | copy-start | bytes 196
  756.3 15.6 %copy-start.8 = (bf16[4,2,128]{2,1,0:T(2,128)(2,1)S(1)}, bf16[4,2,128]{2,1,0:T(2,128)(2,1)}, u32[]{:S(2)}) copy-start(bf16[4,2,128]{2,1,0:T(2,128)(2,1)} %copy-done.7) | copy-start | bytes 6148
  756.3 36.2 %copy-start.4 = (bf16[2,64,256]{2,1,0:T(8,128)(2,1)S(1)}, bf16[2,64,256]{2,1,0:T(8,128)(2,1)}, u32[]{:S(2)}) copy-start(bf16[2,64,256]{2,1,0:T(8,128)(2,1)} %param.21) | copy-start | bytes 196612
  773.8 19.8 %all-to-all-start.3 = ((bf16[4,8,2,2048]{3,1,2,0:T(8,128)(2,1)}), bf16[4,8,2,2048]{3,1,2,0:T(8,128)(2,1)S(1)}, u32[]{:S(2)}, u32[]{:S(2)}) async-start(bf16[4,8,2,2048]{3,1,2,0:T(8,128)(2,1)} %copy.238), calls=%async_computation.3 | async-start | bytes 524288 | tf_op jit(solution)/shard_map/all_to_all | solution.py:144
  793.5 11.0 %all-to-all-start.6 = ((bf16[4,32,2,256]{3,1,2,0:T(8,128)(2,1)}), bf16[4,32,2,256]{3,1,2,0:T(8,128)(2,1)S(1)}, u32[]{:S(2)}, u32[]{:S(2)}) async-start(bf16[4,32,2,256]{3,1,2,0:T(8,128)(2,1)} %bitcast.53), calls=%async_computation.7 | async-start | bytes 262144 | tf_op jit(solution)/shard_map/all_to_all | solution.py:188
Sparse Core Ops, SparseCore 0:
  24.1 21.5 reduce-scatter.1
where the time goes:
time: 823 us; the launch traced here: 816 us
  local copies, waits for them, and re-layouts  468 us (57%)
  other arithmetic  211 us (26%)
  starting transfers between devices  37.4 us (5%)
  matrix products  33 us (4%)
  loops' own time  31.3 us (4%)
  between operations  14.9 us (2%)
  blocking collectives  10.6 us (1%)
  waiting for transfers between devices  10.1 us (1%)
    gather x15, local copies, waits for them, and re-layouts, one_block(): one_score[:, :, :, one_table, :]  169 us
    gather x5, local copies, waits for them, and re-layouts, one_block(): row_values = page_values[t_blk].reshape(block, span, heads_kv, HEAD_WIDTH)  126 us
    reduce_max x5, other arithmetic, one_block(): largest = jnp.max(picked, axis=-1)  106 us
    reduce_sum x5, other arithmetic, one_block(): total = jnp.sum(expo, axis=-1)  95 us
    reshape x5, local copies, waits for them, and re-layouts, one_block(): picked = picked.reshape(block, step_total, heads_kv, group, span)  70.8 us
    reshape x10, local copies, waits for them, and re-layouts, one_block(): whole = whole.reshape(block, step_total, heads_kv, group, pages, page_len)  43.4 us
    another operation x2, loops' own time, pool_attention(): lax.map(one_block, (query.reshape(count // block, block, step_total, -1),...  31.3 us
    dot_general x5, matrix products, one_block(): jnp.einsum('bikgc,bckd->bikgd', weights, row_values, preferred_element_ty...  24.1 us
  transfers between devices with their start and end apart: 9, of which 4 were waited for; matrix products, arithmetic and copies ran while one was open for 86% of the time, Pallas kernels for 0%

commit v1 on v0

v1 whole, which is shorter than its diff:
```python
import functools
import math

import jax
import jax.numpy as jnp
from jax import lax
from jax.experimental import pallas as pl
from jax.experimental.pallas import tpu as pltpu
from jax.sharding import PartitionSpec as P

HEAD_WIDTH = 128

adapter_scale = 2.0
masked_score = -1e30
scale = 1.0 / math.sqrt(HEAD_WIDTH)


def position_counts(table, length, pages, page_len):
    rows, entries = table.shape
    start = lax.broadcasted_iota(jnp.int32, (rows, entries), 1) * page_len
    full = jnp.where(start + page_len <= length, 1.0, 0.0)
    part = jnp.where(start < length, 1.0, 0.0) - full
    span = pages * page_len
    lane = lax.broadcasted_iota(jnp.int32, (rows, span), 1)
    page = lane // page_len
    tail = jnp.where(lane - page * page_len < length % page_len, 1.0, 0.0)
    counts = jnp.zeros((rows, span), jnp.float32)
    for p in range(pages):
        hit = table == p
        whole = jnp.sum(jnp.where(hit, full, 0.0), axis=1, keepdims=True)
        rest = jnp.sum(jnp.where(hit, part, 0.0), axis=1, keepdims=True)
        counts = jnp.where(page == p, whole + rest * tail, counts)
    return counts


def pool_attention(q_ref, keys, values, counts, here, acc_ref, top_ref, sum_ref, group):
    heads = q_ref.shape[1] // HEAD_WIDTH
    for h in range(heads):
        cols = slice(h * HEAD_WIDTH, (h + 1) * HEAD_WIDTH)
        kv = slice(h // group * HEAD_WIDTH, (h // group + 1) * HEAD_WIDTH)
        s = lax.dot_general(
            q_ref[:, cols], keys[:, kv], (((1,), (1,)), ((), ())),
            preferred_element_type=jnp.float32,
        ) * scale
        s = jnp.where(counts > 0.0, s, masked_score)
        top = jnp.max(s, axis=1, keepdims=True)
        weight = jnp.exp(s - top) * counts
        total = jnp.sum(weight, axis=1, keepdims=True)
        mixed = jnp.dot(
            weight.astype(jnp.bfloat16), values[:, kv], preferred_element_type=jnp.float32
        )
        acc_ref[:, cols] = jnp.where(here, mixed, acc_ref[:, cols])
        top_ref[:, h : h + 1] = jnp.where(here, top, top_ref[:, h : h + 1])
        sum_ref[:, h : h + 1] = jnp.where(here, total, sum_ref[:, h : h + 1])


def add_fresh(q_ref, kn_ref, fresh, acc_ref, top_ref, sum_ref, out_ref, group):
    tokens = q_ref.shape[0]
    rows = tokens // 2
    heads = q_ref.shape[1] // HEAD_WIDTH
    second = lax.broadcasted_iota(jnp.int32, (tokens, 1), 0) >= rows
    for k in range(heads // group):
        kv = slice(k * HEAD_WIDTH, (k + 1) * HEAD_WIDTH)
        key_new = kn_ref[:, kv].astype(jnp.float32)
        k0 = jnp.concatenate([key_new[:rows], key_new[:rows]], axis=0)
        k1 = jnp.concatenate([key_new[rows:], key_new[rows:]], axis=0)
        v_new = fresh[:, kv].astype(jnp.float32)
        v0 = jnp.concatenate([v_new[:rows], v_new[:rows]], axis=0)
        v1 = jnp.concatenate([v_new[rows:], v_new[rows:]], axis=0)
        for h in range(k * group, (k + 1) * group):
            cols = slice(h * HEAD_WIDTH, (h + 1) * HEAD_WIDTH)
            q = q_ref[:, cols].astype(jnp.float32)
            s0 = jnp.sum(q * k0, axis=1, keepdims=True) * scale
            s1 = jnp.sum(q * k1, axis=1, keepdims=True) * scale
            s1 = jnp.where(second, s1, masked_score)
            top = top_ref[:, h : h + 1]
            largest = jnp.maximum(top, jnp.maximum(s0, s1))
            keep = jnp.exp(top - largest)
            e0 = jnp.exp(s0 - largest)
            e1 = jnp.exp(s1 - largest)
            total = sum_ref[:, h : h + 1] * keep + e0 + e1
            mixed = acc_ref[:, cols] * keep
            mixed = mixed + e0.astype(jnp.bfloat16).astype(jnp.float32) * v0
            mixed = mixed + e1.astype(jnp.bfloat16).astype(jnp.float32) * v1
            out_ref[:, cols] = (mixed / total).astype(jnp.bfloat16)


def attention_kernel(
    stores, pages, page_len, group,
    q_ref, kn_ref, fresh_ref, table_ref, length_ref, holder_ref, pool_ref, out_ref,
    acc_ref, top_ref, sum_ref,
):
    counts = position_counts(table_ref[...], length_ref[...], pages, page_len)
    counts = jnp.concatenate([counts, counts], axis=0)
    holder = jnp.concatenate([holder_ref[...], holder_ref[...]], axis=0)
    acc_ref[...] = jnp.zeros_like(acc_ref)
    top_ref[...] = jnp.zeros_like(top_ref)
    sum_ref[...] = jnp.zeros_like(sum_ref)

    def step(s, carry):
        here = holder == s
        pool_attention(
            q_ref, pool_ref[s, 0], pool_ref[s, 1], jnp.where(here, counts, 0.0), here,
            acc_ref, top_ref, sum_ref, group,
        )
        return carry

    lax.fori_loop(0, stores, step, 0)
    add_fresh(q_ref, kn_ref, fresh_ref[...], acc_ref, top_ref, sum_ref, out_ref, group)


def per_device(
    hidden,
    queries,
    fresh_rotated_keys,
    value_matrix,
    adapter_down_factors,
    adapter_up_factors,
    adapter_index_rows,
    key_value_pool,
    row_page_table,
    context_length,
    relocated_rows,
    relocated_destination,
):
    stores = lax.axis_size("store")
    me = lax.axis_index("store")
    rows, steps, feats = hidden.shape
    tokens = rows * steps
    width = fresh_rotated_keys.shape[2]
    q_width = queries.shape[2]
    group = q_width // width
    pages, page_len = key_value_pool.shape[1:3]
    span = pages * page_len
    rank = adapter_up_factors.shape[1]
    adapters = adapter_down_factors.shape[0] * stores

    down = lax.all_gather(adapter_down_factors, "store", axis=0, tiled=True)
    up = lax.all_gather(adapter_up_factors, "store", axis=0, tiled=True)
    pool = lax.all_gather(key_value_pool.reshape(2, span, width), "store", axis=0)

    x = hidden.transpose(1, 0, 2).reshape(tokens, feats)
    q = queries.transpose(1, 0, 2).reshape(tokens, q_width)
    kn = fresh_rotated_keys.transpose(1, 0, 2).reshape(tokens, width)
    base = jnp.dot(x, value_matrix, preferred_element_type=jnp.float32)
    base = lax.psum_scatter(
        base.astype(jnp.bfloat16), "tp", scatter_dimension=1, tiled=True
    ).astype(jnp.float32)
    named = jnp.concatenate([adapter_index_rows, adapter_index_rows], axis=0)
    chosen = named == jnp.arange(adapters, dtype=jnp.int32)[None, :]
    middle = jnp.einsum("tf,afb->tab", x, down, preferred_element_type=jnp.float32)
    middle = jnp.sum(jnp.where(chosen[:, :, None], middle, 0.0), axis=1)
    middle = lax.psum(middle.astype(jnp.bfloat16), "tp")
    spread = jnp.where(chosen[:, :, None], middle[:, None, :], 0).reshape(tokens, adapters * rank)
    term = jnp.dot(
        spread, up.reshape(adapters * rank, width), preferred_element_type=jnp.float32
    )
    fresh = (base + adapter_scale * term).astype(jnp.bfloat16)

    hits = relocated_rows[None, :] == jnp.arange(rows, dtype=jnp.int32)[:, None]
    away = jnp.sum(jnp.where(hits, relocated_destination[:, 0][None, :] - me, 0), axis=1)
    holder = (me + away)[:, None]

    attention = pl.pallas_call(
        functools.partial(attention_kernel, stores, pages, page_len, group),
        out_shape=jax.ShapeDtypeStruct((tokens, q_width), jnp.bfloat16),
        in_specs=[pl.BlockSpec(memory_space=pltpu.VMEM)] * 7,
        out_specs=pl.BlockSpec(memory_space=pltpu.VMEM),
        scratch_shapes=[
            pltpu.VMEM((tokens, q_width), jnp.float32),
            pltpu.VMEM((tokens, q_width // HEAD_WIDTH), jnp.float32),
            pltpu.VMEM((tokens, q_width // HEAD_WIDTH), jnp.float32),
        ],
        compiler_params=pltpu.CompilerParams(vmem_limit_bytes=48 * 1024 * 1024),
    )(q, kn, fresh, row_page_table, context_length[:, None], holder, pool)
    return (
        attention.reshape(steps, rows, q_width).transpose(1, 0, 2),
        fresh.reshape(steps, rows, width).transpose(1, 0, 2),
    )


def solution(mesh):
    placed = (
        P(("grp", "store"), None, "tp"),
        P(("grp", "store"), None, "tp"),
        P(("grp", "store"), None, "tp"),
        P("tp", None),
        P("store", "tp", None),
        P("store", None, "tp"),
        P(("grp", "store"), None),
        P(None, ("grp", "store"), None, "tp"),
        P(("grp", "store"), None),
        P(("grp", "store")),
        P(("grp", "store")),
        P(("grp", "store"), None),
    )
    return jax.shard_map(
        per_device,
        mesh=mesh,
        in_specs=placed,
        out_specs=(P(("grp", "store"), None, "tp"), P(("grp", "store"), None, "tp")),
        check_vma=False,
    )
```

time: 823 us -> 127 us (0.15)
  local copies, waits for them, and re-layouts: 468 us -> 4.85 us
  other arithmetic: 211 us -> 0.21 us
  starting transfers between devices: 37.4 us -> 0.12 us
  waiting for transfers between devices: 10.1 us -> 45 us
  loops' own time: 31.3 us -> 0 us
  matrix products: 33 us -> 7.03 us
  Pallas kernels: 0 us -> 25 us
  blocking collectives: 10.6 us -> 28.8 us
    gather x29 -> x0, local copies, waits for them, and re-layouts: 305 us -> none  [the longest x15 169 us: one_block(): one_score[:, :, :, one_table, :]]
    reshape x28 -> x2, local copies, waits for them, and re-layouts: 122 us -> 2.03 us  [the longest x1 1.33 us: per_device(): attention.reshape(steps, rows, q_width).transpose(1, 0, 2)]
    reduce_max x5 -> x0, other arithmetic: 106 us -> none  [one_block(): largest = jnp.max(picked, axis=-1)]
    reduce_sum x8 -> x2, other arithmetic: 96.5 us -> 0.12 us  [the longest x1 0.09 us: per_device(): jnp.sum(jnp.where(hits, relocated_destination[:, 0][None, :] - me, 0), ax...]
    all_gather x0 -> x2, waiting for transfers between devices: none -> 43.6 us  [the longest x1 29.1 us: per_device(): down = lax.all_gather(adapter_down_factors, 'store', axis=0, tiled=True)]
    all_to_all x8 -> x0, starting transfers between devices: 37.4 us -> none  [the longest x1 6.32 us: per_device(): lax.all_to_all(moved_l, 'store', split_axis=0, concat_axis=0, tiled=True)]
    another operation x2 -> x0, loops' own time: 31.3 us -> none  [pool_attention(): lax.map(one_block, (query.reshape(count // block, block, step_total, -1),...]
    dot_general x15 -> x2, matrix products: 33 us -> 4.72 us  [the longest x1 3.65 us: per_device(): base = jnp.dot(x, value_matrix, preferred_element_type=jnp.float32)]
  transfers between devices with their start and end apart: 9 -> 3, of which waited for: 4 -> 2; matrix products, arithmetic and copies ran while one was open for 86% -> 7% of each run, Pallas kernels for 0% -> 0%
where the time goes in v1:
time: 127 us
  waiting for transfers between devices  45 us (35%)
  blocking collectives  28.8 us (23%)
  Pallas kernels  25 us (20%)
  between operations  15.6 us (12%)
  matrix products  7.03 us (6%)
  local copies, waits for them, and re-layouts  4.85 us (4%)
    all_gather x1, waiting for transfers between devices, per_device(): down = lax.all_gather(adapter_down_factors, 'store', axis=0, tiled=True)  29.1 us
    pallas_call x1, Pallas kernels, per_device(): pl.pallas_call(functools.partial(attention_kernel, stores, pages, page_le...  25 us
    all_gather x1, blocking collectives, per_device(): up = lax.all_gather(adapter_up_factors, 'store', axis=0, tiled=True)  17.7 us
    all_gather x1, waiting for transfers between devices, per_device(): lax.all_gather(key_value_pool.reshape(2, span, width), 'store', axis=0)  14.5 us
    psum x1, blocking collectives, per_device(): middle = lax.psum(middle.astype(jnp.bfloat16), 'tp')  11.2 us
    dot_general x1, matrix products, per_device(): base = jnp.dot(x, value_matrix, preferred_element_type=jnp.float32)  3.65 us
  transfers between devices with their start and end apart: 3, of which 2 were waited for; matrix products, arithmetic and copies ran while one was open for 7% of the time, Pallas kernels for 0%

profile of v1, /device:TPU:0, one launch (start us, length us, event | category | flops | bytes accessed | tf_op | source)
XLA Modules:
  0.0 126.7 jit_solution(55692457180313544)
XLA Ops:
  8.0 0.0 copy-start.6
  8.0 0.0 copy-start.7
  8.0 0.0 copy-start.2
  8.0 0.0 copy-start.4
  8.0 0.0 copy-start.5
  8.0 0.0 copy-start.3
  8.1 0.0 all-gather.3.cloned.1.call-start
  8.1 0.7 all-gather.3.cloned.1.call-update
  8.8 0.0 copy-start.8
  8.8 0.0 reduce-scatter.2.cloned.1.call-start
  8.9 1.2 copy.36
  10.1 0.0 copy-start.1
  10.1 3.7 %convolution_convert_fusion = bf16[128,1024]{1,0:T(8,128)(2,1)} fusion(bf16[128,2048]{1,0:T(8,128)(2,1)S(1)} %bitcast.44, bf16[2048,1024]{1,0:T(8,128)(2,1)} %param.15), kind=kOutput, calls=%fused_computation | convolution fusion | flops 537001984 | bytes 4980736 | tf_op jit(solution)/shard_map/dot_general | solution.py:145
  13.7 0.0 reduce-scatter.2.cloned.1.call-update
  13.7 0.0 all-gather.5.cloned.1.call-start
  13.8 0.7 all-gather.5.cloned.1.call-update
  14.5 0.0 copy-done.6
  14.5 0.0 copy-done.7
  14.5 0.1 select_reduce_fusion.1
  14.6 0.1 copy.38.holder_ref
  14.7 0.0 copy-done.2
  14.7 0.2 copy.34
  14.9 0.0 copy-done.4
  14.9 0.0 copy-done.5
  14.9 0.1 copy.37.length_ref
  15.0 0.0 copy-done.3
  15.0 17.7 %all_gather.10 = bf16[8,64,256]{2,1,0:T(8,128)(2,1)S(1)} all-gather(bf16[2,64,256]{2,1,0:T(8,128)(2,1)S(1)} %copy-done.3), channel_id=1, replica_groups=mesh['grp'=2,'store'=4,'tp'=4] {'store'}, dimensions={0}, use_global_device_ids=true | all-gather | bytes 327680 | tf_op jit(solution)/shard_map/all_gather | solution.py:139
  32.7 0.0 copy-done.8
  32.7 0.1 add_bitcast_fusion
  32.8 29.1 %all-gather.3.cloned.1.call-done = bf16[8,2048,64]{1,2,0:T(8,128)(2,1)} async-done(((bf16[2,2048,64]{1,2,0:T(8,128)(2,1)}), bf16[8,2048,64]{1,2,0:T(8,128)(2,1)}) %all-gather.3.cloned.1.call-update) | async-done | bytes 2097168 | tf_op jit(solution)/shard_map/all_gather | solution.py:138
  61.9 2.3 %fusion.8 = f32[128,512]{0,1:S(1)} fusion(bf16[128,2048]{1,0:T(8,128)(2,1)S(1)} %bitcast.45, bf16[2048,512]{0,1:T(8,128)(2,1)} %bitcast.46), kind=kOutput, calls=%fused_computation.19 | convolution fusion | flops 268435456 | bytes 2883584
  64.2 11.2 %psum.7 = bf16[128,64]{0,1:T(8,128)(2,1)S(1)} all-reduce(bf16[128,64]{0,1:T(8,128)(2,1)S(1)} %select_reduce_fusion), channel_id=1, replica_groups=mesh['grp'=2,'store'=4,'tp'=4] {'tp'}, use_global_device_ids=true, to_apply=%region_2.3 | all-reduce | flops 8192 | bytes 32768 | tf_op jit(solution)/shard_map/psum | solution.py:153
  75.4 0.0 reduce-scatter.2.cloned.1.call-done
  75.4 1.1 fusion.2.fresh_ref
  76.4 14.5 %all-gather.5.cloned.1.call-done.pool_ref = bf16[4,2,256,256]{3,2,1,0:T(8,128)(2,1)} async-done(((bf16[1,2,256,256]{3,2,1,0:T(8,128)(2,1)}), bf16[4,2,256,256]{3,2,1,0:T(8,128)(2,1)}) %all-gather.5.cloned.1.call-update) | async-done | bytes 1048592 | tf_op jit(solution)/shard_map/all_gather | solution.py:140
  91.0 0.0 copy-done.1
  91.0 0.0 copy-start
  91.0 1.2 copy-done
  92.2 25.0 %shard_map.131 = bf16[128,2048]{1,0:T(8,128)(2,1)S(1)} custom-call(bf16[128,2048]{1,0:T(8,128)(2,1)S(1)} %bitcast.40, bf16[128,256]{1,0:T(8,128)(2,1)S(1)} %bitcast.42, bf16[128,256]{1,0:T(8,128)(2,1)S(1)} %fusion.2.fresh_ref, s32[64,64]{1,0:T(8,128)S(1)} %copy-done.1, s32[64,1]{1,0:T(8,128)S(1)} %copy.37.length_ref, s32[64,1]{1,0:T(8,128)S(1)} %copy.38.holder_ref, ...), custom_call_target="tpu_custom_call" | custom-call | tf_op jit(solution)/shard_map/pallas_call | solution.py:164
  117.2 1.3 %copy.43 = bf16[2,64,2048]{2,0,1:T(2,128)(2,1)} copy(bf16[2,64,2048]{2,1,0:T(8,128)(2,1)S(1)} %bitcast.41) | data formatting | bytes 1048576 | tf_op jit(solution)/shard_map/reshape | solution.py:177
  118.5 0.7 copy.44
  (5 shorter events, 0.1 us)
Async XLA Ops:
  8.0 6.5 %copy-start.6 = (s32[16,1]{0,1:T(1,128)S(1)}, s32[16,1]{0,1:T(1,128)}, u32[]{:S(2)}) copy-start(s32[16,1]{0,1:T(1,128)} %param.23) | copy-start | bytes 196
  8.0 6.5 %copy-start.7 = (s32[16]{0:T(128)S(1)}, s32[16]{0:T(128)}, u32[]{:S(2)}) copy-start(s32[16]{0:T(128)} %param.22) | copy-start | bytes 196
  8.0 6.7 %copy-start.2 = (bf16[64,2,2048]{2,1,0:T(2,128)(2,1)S(1)}, bf16[64,2,2048]{2,1,0:T(2,128)(2,1)}, u32[]{:S(2)}) copy-start(bf16[64,2,2048]{2,1,0:T(2,128)(2,1)} %param.13) | copy-start | bytes 1572868
  8.0 6.9 %copy-start.4 = (bf16[64,2,256]{2,1,0:T(2,128)(2,1)S(1)}, bf16[64,2,256]{2,1,0:T(2,128)(2,1)}, u32[]{:S(2)}) copy-start(bf16[64,2,256]{2,1,0:T(2,128)(2,1)} %param.14) | copy-start | bytes 196612
  8.0 6.9 %copy-start.5 = (s32[64]{0:T(128)S(1)}, s32[64]{0:T(128)}, u32[]{:S(2)}) copy-start(s32[64]{0:T(128)} %param.21) | copy-start | bytes 772
  8.0 7.0 %copy-start.3 = (bf16[2,64,256]{2,1,0:T(8,128)(2,1)S(1)}, bf16[2,64,256]{2,1,0:T(8,128)(2,1)}, u32[]{:S(2)}) copy-start(bf16[2,64,256]{2,1,0:T(8,128)(2,1)} %param.17) | copy-start | bytes 196612
  8.1 53.8 %all-gather.3.cloned.1.call-start = ((), (), s32[]{:S(2)}) async-start(), calls=%async_computation.2 | async-start | bytes 2621440 | tf_op jit(solution)/shard_map/all_gather | solution.py:138
  8.8 23.9 %copy-start.8 = (s32[64,1]{0,1:T(1,128)S(1)}, s32[64,1]{0,1:T(1,128)}, u32[]{:S(2)}) copy-start(s32[64,1]{0,1:T(1,128)} %param.18) | copy-start | bytes 772
  8.8 66.6 %reduce-scatter.2.cloned.1.call-start = ((), (), s32[]{:S(2)}) async-start(), calls=%async_computation.1 | async-start | bytes 327680 | tf_op jit(solution)/shard_map/reduce_scatter | solution.py:146
  10.1 80.9 %copy-start.1 = (s32[64,64]{1,0:T(8,128)S(1)}, s32[64,64]{1,0:T(8,128)}, u32[]{:S(2)}) copy-start(s32[64,64]{1,0:T(8,128)} %table_ref.1) | copy-start | bytes 49156
  13.7 77.2 %all-gather.5.cloned.1.call-start = ((), (), s32[]{:S(2)}) async-start(), calls=%async_computation.3 | async-start | bytes 1310720 | tf_op jit(solution)/shard_map/all_gather | solution.py:140
  91.0 1.2 copy-start
Sparse Core Ops, SparseCore 0:
  10.5 51.2 all-gather.2
  63.5 27.4 all-gather.4
Sparse Core Ops, SparseCore 1:
  13.8 22.7 reduce-scatter.1

commit v2 on v1

--- a/solution.py
+++ b/solution.py
@@ -85,28 +85,221 @@
             out_ref[:, cols] = (mixed / total).astype(jnp.bfloat16)
 
 
-def attention_kernel(
-    stores, pages, page_len, group,
-    q_ref, kn_ref, fresh_ref, table_ref, length_ref, holder_ref, pool_ref, out_ref,
-    acc_ref, top_ref, sum_ref,
+def serving_kernel(
+    stores, parts, pages, page_len, group,
+    x_ref, q_ref, kn_ref, table_ref, length_ref, holder_ref, named_ref,
+    value_hbm, down_hbm, up_hbm, pool_hbm,
+    out_ref, fresh_ref,
+    value_ref, down_ref, up_ref, pool_ref, base_send, base_recv, mid_send, mid_recv,
+    acc_ref, top_ref, sum_ref, count_ref,
+    local_sem, line_send, line_recv, pair_send, pair_recv, base_ssem, base_rsem,
+    mid_ssem, mid_rsem,
 ):
+    me = lax.axis_index("store")
+    half = lax.axis_index("grp")
+    tp = lax.axis_index("tp")
+    tokens = x_ref.shape[0]
+    width = kn_ref.shape[1]
+    resident = down_ref.shape[1] * down_ref.shape[2]
+    mesh_ids = pl.DeviceIdType.MESH
+
+    loads = [
+        pltpu.make_async_copy(down_hbm, down_ref.at[me], local_sem.at[0]),
+        pltpu.make_async_copy(up_hbm, up_ref.at[me], local_sem.at[1]),
+        pltpu.make_async_copy(pool_hbm, pool_ref.at[me], local_sem.at[2]),
+        pltpu.make_async_copy(value_hbm, value_ref, local_sem.at[3]),
+    ]
+    for load in loads:
+        load.start()
+
+    barrier = pltpu.get_barrier_semaphore()
+    for d in range(1, parts):
+        pl.semaphore_signal(
+            barrier, inc=1, device_id={"tp": lax.rem(tp + d, parts)}, device_id_type=mesh_ids
+        )
+    pl.semaphore_signal(barrier, inc=1, device_id={"grp": 1 - half}, device_id_type=mesh_ids)
+
+    @pl.when(me > 0)
+    def _():
+        pl.semaphore_signal(barrier, inc=1, device_id={"store": me - 1}, device_id_type=mesh_ids)
+
+    @pl.when(me < stores - 1)
+    def _():
+        pl.semaphore_signal(barrier, inc=1, device_id={"store": me + 1}, device_id_type=mesh_ids)
+
+    ends = jnp.where(me > 0, 1, 0) + jnp.where(me < stores - 1, 1, 0)
+    pl.semaphore_wait(barrier, parts + ends)
+
+    for load in loads[:3]:
+        load.wait()
+
+    def line(stream, slot, way, t, to):
+        ref = (down_ref.at[slot, half], up_ref.at[slot, half], pool_ref.at[slot])[stream]
+        return pltpu.make_async_remote_copy(
+            src_ref=ref, dst_ref=ref,
+            send_sem=line_send.at[stream, way, t], recv_sem=line_recv.at[stream, slot],
+            device_id={"store": to}, device_id_type=mesh_ids,
+        )
+
+    def pair(stream, slot, which):
+        ref = (down_ref, up_ref)[stream].at[slot, which]
+        return pltpu.make_async_remote_copy(
+            src_ref=ref, dst_ref=ref,
+            send_sem=pair_send.at[stream, slot], recv_sem=pair_recv.at[stream, slot],
+            device_id={"grp": 1 - half}, device_id_type=mesh_ids,
+        )
+
+    def sends(t, act):
+        @pl.when((me - t >= 0) & (me < stores - 1))
+        def _():
+            for stream in range(3):
+                act(line(stream, me - t, 0, t, me + 1))
+
+        @pl.when((me + t < stores) & (me > 0))
+        def _():
+            for stream in range(3):
+                act(line(stream, me + t, 1, t, me - 1))
+
+    def arrivals(t, streams, swap):
+        @pl.when(me - 1 - t >= 0)
+        def _():
+            for stream in streams:
+                line(stream, me - 1 - t, 0, t, me - 1).wait_recv()
+                if swap:
+                    pair(stream, me - 1 - t, half).start()
+
+        @pl.when(me + 1 + t < stores)
+        def _():
+            for stream in streams:
+                line(stream, me + 1 + t, 1, t, me + 1).wait_recv()
+                if swap:
+                    pair(stream, me + 1 + t, half).start()
+
+    def attend(slot):
+        holder = jnp.concatenate([holder_ref[...], holder_ref[...]], axis=0)
+        here = holder == slot
+        pool_attention(
+            q_ref, pool_ref[slot, 0], pool_ref[slot, 1], jnp.where(here, count_ref[...], 0.0),
+            here, acc_ref, top_ref, sum_ref, group,
+        )
+
+    def attend_pair(t):
+        @pl.when(me - t >= 0)
+        def _():
+            attend(me - t)
+
+        @pl.when(me + t < stores)
+        def _():
+            attend(me + t)
+
+    sends(0, lambda copy: copy.start())
+
+    loads[3].wait()
+    for c in range(parts):
+        base_send[c] = jnp.dot(
+            x_ref[...], value_ref[:, c * width : (c + 1) * width],
+            preferred_element_type=jnp.float32,
+        ).astype(jnp.bfloat16)
+
+    def base_copy(d):
+        to = lax.rem(tp + d, parts)
+        return pltpu.make_async_remote_copy(
+            src_ref=base_send.at[to], dst_ref=base_recv.at[d - 1],
+            send_sem=base_ssem.at[d - 1], recv_sem=base_rsem.at[d - 1],
+            device_id={"tp": to}, device_id_type=mesh_ids,
+        )
+
+    def mid_copy(d):
+        return pltpu.make_async_remote_copy(
+            src_ref=mid_send, dst_ref=mid_recv.at[d - 1],
+            send_sem=mid_ssem.at[d - 1], recv_sem=mid_rsem.at[d - 1],
+            device_id={"tp": lax.rem(tp + d, parts)}, device_id_type=mesh_ids,
+        )
+
+    for d in range(1, parts):
+        base_copy(d).start()
+
     counts = position_counts(table_ref[...], length_ref[...], pages, page_len)
-    counts = jnp.concatenate([counts, counts], axis=0)
-    holder = jnp.concatenate([holder_ref[...], holder_ref[...]], axis=0)
+    count_ref[...] = jnp.concatenate([counts, counts], axis=0)
     acc_ref[...] = jnp.zeros_like(acc_ref)
     top_ref[...] = jnp.zeros_like(top_ref)
     sum_ref[...] = jnp.zeros_like(sum_ref)
-
-    def step(s, carry):
-        here = holder == s
-        pool_attention(
-            q_ref, pool_ref[s, 0], pool_ref[s, 1], jnp.where(here, counts, 0.0), here,
-            acc_ref, top_ref, sum_ref, group,
-        )
+    attend(me)
+    arrivals(0, (0, 1), True)
+    arrivals(0, (2,), False)
+
+    def step(t, carry):
+        sends(t, lambda copy: copy.start())
+        attend_pair(t)
+        arrivals(t, (0, 1), True)
+
+        @pl.when(t < stores - 2)
+        def _():
+            arrivals(t, (2,), False)
+
         return carry
 
-    lax.fori_loop(0, stores, step, 0)
-    add_fresh(q_ref, kn_ref, fresh_ref[...], acc_ref, top_ref, sum_ref, out_ref, group)
+    lax.fori_loop(1, stores - 1, step, 0)
+
+    named = jnp.concatenate([named_ref[...], named_ref[...]], axis=0)
+    lane = lax.broadcasted_iota(jnp.int32, (tokens, resident), 1)
+    own_lane = lane // (resident // 2)
+
+    def middle(k, total):
+        @pl.when(k != me)
+        def _():
+            for stream in range(2):
+                pair(stream, k, 1 - half).wait_recv()
+
+        product = lax.dot_general(
+            x_ref[...], down_ref[k].reshape(resident, down_ref.shape[3]),
+            (((1,), (1,)), ((), ())), preferred_element_type=jnp.float32,
+        )
+        return total + jnp.where(named == own_lane + 2 * k, product, 0.0)
+
+    mid = lax.fori_loop(0, stores, middle, jnp.zeros((tokens, resident), jnp.float32))
+    mid_send[...] = mid.astype(jnp.bfloat16)
+    for d in range(1, parts):
+        mid_copy(d).start()
+
+    arrivals(stores - 2, (2,), False)
+    attend_pair(stores - 1)
+
+    for d in range(1, parts):
+        base_copy(d).wait()
+        mid_copy(d).wait()
+    base = base_send[tp].astype(jnp.float32)
+    mid = mid_send[...].astype(jnp.float32)
+    for d in range(1, parts):
+        base = base + base_recv[d - 1].astype(jnp.float32)
+        mid = mid + mid_recv[d - 1].astype(jnp.float32)
+
+    def upward(k, total):
+        chosen = jnp.where(named // 2 == k, mid, 0.0).astype(jnp.bfloat16)
+        return total + jnp.dot(
+            chosen, up_ref[k].reshape(resident, width), preferred_element_type=jnp.float32
+        )
+
+    term = lax.fori_loop(0, stores, upward, jnp.zeros((tokens, width), jnp.float32))
+    fresh = (base + adapter_scale * term).astype(jnp.bfloat16)
+    fresh_ref[...] = fresh
+    add_fresh(q_ref, kn_ref, fresh, acc_ref, top_ref, sum_ref, out_ref, group)
+
+    def finish(t, carry):
+        sends(t, lambda copy: copy.wait_send())
+        return carry
+
+    lax.fori_loop(0, stores - 1, finish, 0)
+
+    def finish_pair(k, carry):
+        @pl.when(k != me)
+        def _():
+            for stream in range(2):
+                pair(stream, k, half).wait_send()
+
+        return carry
+
+    lax.fori_loop(0, stores, finish_pair, 0)
 
 
 def per_device(
@@ -132,47 +325,61 @@
     group = q_width // width
     pages, page_len = key_value_pool.shape[1:3]
     span = pages * page_len
-    rank = adapter_up_factors.shape[1]
-    adapters = adapter_down_factors.shape[0] * stores
-
-    down = lax.all_gather(adapter_down_factors, "store", axis=0, tiled=True)
-    up = lax.all_gather(adapter_up_factors, "store", axis=0, tiled=True)
-    pool = lax.all_gather(key_value_pool.reshape(2, span, width), "store", axis=0)
+    parts = lax.axis_size("tp")
+    resident = adapter_up_factors.shape[0] * adapter_up_factors.shape[1]
 
     x = hidden.transpose(1, 0, 2).reshape(tokens, feats)
     q = queries.transpose(1, 0, 2).reshape(tokens, q_width)
     kn = fresh_rotated_keys.transpose(1, 0, 2).reshape(tokens, width)
-    base = jnp.dot(x, value_matrix, preferred_element_type=jnp.float32)
-    base = lax.psum_scatter(
-        base.astype(jnp.bfloat16), "tp", scatter_dimension=1, tiled=True
-    ).astype(jnp.float32)
-    named = jnp.concatenate([adapter_index_rows, adapter_index_rows], axis=0)
-    chosen = named == jnp.arange(adapters, dtype=jnp.int32)[None, :]
-    middle = jnp.einsum("tf,afb->tab", x, down, preferred_element_type=jnp.float32)
-    middle = jnp.sum(jnp.where(chosen[:, :, None], middle, 0.0), axis=1)
-    middle = lax.psum(middle.astype(jnp.bfloat16), "tp")
-    spread = jnp.where(chosen[:, :, None], middle[:, None, :], 0).reshape(tokens, adapters * rank)
-    term = jnp.dot(
-        spread, up.reshape(adapters * rank, width), preferred_element_type=jnp.float32
-    )
-    fresh = (base + adapter_scale * term).astype(jnp.bfloat16)
+    down = adapter_down_factors.transpose(0, 2, 1).reshape(2, resident // 2, feats)
+    up = adapter_up_factors.reshape(2, resident // 2, width)
+    pool = key_value_pool.reshape(2, span, width)
 
     hits = relocated_rows[None, :] == jnp.arange(rows, dtype=jnp.int32)[:, None]
     away = jnp.sum(jnp.where(hits, relocated_destination[:, 0][None, :] - me, 0), axis=1)
     holder = (me + away)[:, None]
 
-    attention = pl.pallas_call(
-        functools.partial(attention_kernel, stores, pages, page_len, group),
-        out_shape=jax.ShapeDtypeStruct((tokens, q_width), jnp.bfloat16),
-        in_specs=[pl.BlockSpec(memory_space=pltpu.VMEM)] * 7,
-        out_specs=pl.BlockSpec(memory_space=pltpu.VMEM),
+    heads = q_width // HEAD_WIDTH
+    dma = pltpu.SemaphoreType.DMA
+    attention, fresh = pl.pallas_call(
+        functools.partial(serving_kernel, stores, parts, pages, page_len, group),
+        out_shape=(
+            jax.ShapeDtypeStruct((tokens, q_width), jnp.bfloat16),
+            jax.ShapeDtypeStruct((tokens, width), jnp.bfloat16),
+        ),
+        in_specs=[pl.BlockSpec(memory_space=pltpu.VMEM)] * 7
+        + [pl.BlockSpec(memory_space=pl.ANY)] * 4,
+        out_specs=[pl.BlockSpec(memory_space=pltpu.VMEM)] * 2,
         scratch_shapes=[
+            pltpu.VMEM(value_matrix.shape, jnp.bfloat16),
+            pltpu.VMEM((stores,) + down.shape, jnp.bfloat16),
+            pltpu.VMEM((stores,) + up.shape, jnp.bfloat16),
+            pltpu.VMEM((stores,) + pool.shape, jnp.bfloat16),
+            pltpu.VMEM((parts, tokens, width), jnp.bfloat16),
+            pltpu.VMEM((parts - 1, tokens, width), jnp.bfloat16),
+            pltpu.VMEM((tokens, resident), jnp.bfloat16),
+            pltpu.VMEM((parts - 1, tokens, resident), jnp.bfloat16),
             pltpu.VMEM((tokens, q_width), jnp.float32),
-            pltpu.VMEM((tokens, q_width // HEAD_WIDTH), jnp.float32),
-            pltpu.VMEM((tokens, q_width // HEAD_WIDTH), jnp.float32),
+            pltpu.VMEM((tokens, heads), jnp.float32),
+            pltpu.VMEM((tokens, heads), jnp.float32),
+            pltpu.VMEM((tokens, span), jnp.float32),
+            dma((4,)),
+            dma((3, 2, stores)),
+            dma((3, stores)),
+            dma((2, stores)),
+            dma((2, stores)),
+            dma((parts - 1,)),
+            dma((parts - 1,)),
+            dma((parts - 1,)),
+            dma((parts - 1,)),
         ],
-        compiler_params=pltpu.CompilerParams(vmem_limit_bytes=48 * 1024 * 1024),
-    )(q, kn, fresh, row_page_table, context_length[:, None], holder, pool)
+        compiler_params=pltpu.CompilerParams(
+            collective_id=0, has_side_effects=True, vmem_limit_bytes=48 * 1024 * 1024
+        ),
+    )(
+        x, q, kn, row_page_table, context_length[:, None], holder, adapter_index_rows,
+        value_matrix, down, up, pool,
+    )
     return (
         attention.reshape(steps, rows, q_width).transpose(1, 0, 2),
         fresh.reshape(steps, rows, width).transpose(1, 0, 2),

time: 127 us -> 70.1 us (0.55)
  waiting for transfers between devices: 45 us -> 0 us
  Pallas kernels: 25 us -> 57.1 us
  blocking collectives: 28.8 us -> 0 us
  between operations: 15.6 us -> 0.67 us
  matrix products: 7.03 us -> 0 us
  local copies, waits for them, and re-layouts: 4.85 us -> 10.4 us
    all_gather x2 -> x0, waiting for transfers between devices: 43.6 us -> none  [the longest x1 29.1 us: per_device(): down = lax.all_gather(adapter_down_factors, 'store', axis=0, tiled=True)]
    pallas_call x1, Pallas kernels: 25 us -> 57.1 us  [per_device(): pl.pallas_call(functools.partial(serving_kernel, stores, parts, pages, pa...]
    all_gather x1 -> x0, blocking collectives: 17.7 us -> none  [per_device(): up = lax.all_gather(adapter_up_factors, 'store', axis=0, tiled=True)]
    psum x1 -> x0, blocking collectives: 11.2 us -> none  [per_device(): middle = lax.psum(middle.astype(jnp.bfloat16), 'tp')]
    dot_general x2 -> x0, matrix products: 4.72 us -> none  [the longest x1 3.65 us: per_device(): base = jnp.dot(x, value_matrix, preferred_element_type=jnp.float32)]
    unnamed x1 -> x0, matrix products: 2.31 us -> none
    unnamed x19 -> x9, local copies, waits for them, and re-layouts: 2.46 us -> 4.33 us
    unnamed x3 -> x0, waiting for transfers between devices: 1.39 us -> none
  transfers between devices with their start and end apart: 3 -> 0, of which waited for: 2 -> 0; matrix products, arithmetic and copies ran while one was open for 7% -> 0% of each run, Pallas kernels for 0% -> 0%
where the time goes in v2:
time: 70.1 us; the launch traced here: 69.6 us
  Pallas kernels  57.1 us (81%)
  local copies, waits for them, and re-layouts  10.4 us (15%)
  other arithmetic  1.41 us (2%)
    pallas_call x1, Pallas kernels, per_device(): pl.pallas_call(functools.partial(serving_kernel, stores, parts, pages, pa...  57.1 us
    unnamed x9, local copies, waits for them, and re-layouts  4.33 us

profile of v2, /device:TPU:0, one launch (start us, length us, event | category | flops | bytes accessed | tf_op | source)
XLA Modules:
  0.0 69.6 jit_solution(10346687322743102813)
XLA Ops:
  0.6 0.7 subtract_bitcast_fusion
  1.3 0.7 %select_reduce_fusion = s32[64]{0:T(128)S(1)} fusion(s32[16]{0:T(128)S(1)} %subtract_bitcast_fusion, s32[16]{0:T(128)} %param.22), kind=kLoop, calls=%fused_computation.2 | loop fusion | flops 3008 | bytes 384 | tf_op jit(solution)/shard_map/reduce_sum | solution.py:339
  2.0 0.1 copy.26.holder_ref
  2.1 0.7 %copy.27.named_ref = s32[64,1]{1,0:T(8,128)S(1)} copy(s32[64,1]{0,1:T(1,128)} %param.18) | data formatting | bytes 512 | tf_op args[6]
  2.9 0.7 %copy.25.length_ref = s32[64,1]{1,0:T(8,128)S(1)} copy(s32[64,1]{0,1:T(1,128)} %bitcast.33) | data formatting | bytes 512 | tf_op jit(solution)/shard_map/broadcast_in_dim | solution.py:380
  3.6 0.8 %copy.24 = bf16[2,64,256]{2,1,0:T(8,128)(2,1)S(1)} copy(bf16[2,64,256]{2,0,1:T(2,128)(2,1)} %bitcast.31) | data formatting | bytes 131072 | tf_op jit(solution)/shard_map/transpose | solution.py:333
  4.5 1.2 %copy.22 = bf16[2,64,2048]{2,1,0:T(8,128)(2,1)S(1)} copy(bf16[2,64,2048]{2,0,1:T(2,128)(2,1)} %bitcast.28) | data formatting | bytes 1048576 | tf_op jit(solution)/shard_map/transpose | solution.py:331
  5.7 1.2 %copy.23 = bf16[2,64,2048]{2,1,0:T(8,128)(2,1)S(1)} copy(bf16[2,64,2048]{2,0,1:T(2,128)(2,1)} %bitcast.29) | data formatting | bytes 1048576 | tf_op jit(solution)/shard_map/transpose | solution.py:332
  6.9 0.0 copy-start
  6.9 1.0 %copy-done = bf16[2,2048,64]{1,2,0:T(8,128)(2,1)S(1)} copy-done((bf16[2,2048,64]{1,2,0:T(8,128)(2,1)S(1)}, bf16[2,2048,64]{1,2,0:T(8,128)(2,1)}, u32[]{:S(2)}) %copy-start) | copy-done | bytes 524312
  7.9 0.0 copy-start.1
  7.9 0.9 %copy-done.1 = bf16[2,16,16,256]{3,2,1,0:T(8,128)(2,1)S(1)} copy-done((bf16[2,16,16,256]{3,2,1,0:T(8,128)(2,1)S(1)}, bf16[2,16,16,256]{3,2,1,0:T(8,128)(2,1)}, u32[]{:S(2)}) %copy-start.1) | copy-done | bytes 262168
  8.9 0.0 copy-start.2
  8.9 0.8 %copy-done.2 = bf16[2,64,256]{2,1,0:T(8,128)(2,1)S(1)} copy-done((bf16[2,64,256]{2,1,0:T(8,128)(2,1)S(1)}, bf16[2,64,256]{2,1,0:T(8,128)(2,1)}, u32[]{:S(2)}) %copy-start.2) | copy-done | bytes 65560
  9.7 0.0 copy-start.3
  9.7 0.8 %copy-done.3 = s32[64,64]{1,0:T(8,128)S(1)} copy-done((s32[64,64]{1,0:T(8,128)S(1)}, s32[64,64]{1,0:T(8,128)}, u32[]{:S(2)}) %copy-start.3) | copy-done | bytes 16408
  10.5 57.1 %shard_map.131 = (bf16[128,2048]{1,0:T(8,128)(2,1)S(1)}, bf16[128,256]{1,0:T(8,128)(2,1)S(1)}) custom-call(bf16[128,2048]{1,0:T(8,128)(2,1)S(1)} %bitcast.21, bf16[128,2048]{1,0:T(8,128)(2,1)S(1)} %bitcast.22, bf16[128,256]{1,0:T(8,128)(2,1)S(1)} %bitcast.25, s32[64,64]{1,0:T(8,128)S(1)} %copy-done.3, s32[64,1]{1,0:T(8,128)S(1)} %copy.25.length_ref, ...), custom_call_target="tpu_custom_call" | custom-call | tf_op jit(solution)/shard_map/pallas_call | solution.py:344
  67.6 1.3 %copy.32 = bf16[2,64,2048]{2,0,1:T(2,128)(2,1)} copy(bf16[2,64,2048]{2,1,0:T(8,128)(2,1)S(1)} %bitcast.24) | data formatting | bytes 1048576 | tf_op jit(solution)/shard_map/reshape | solution.py:384
  68.9 0.7 %copy.33 = bf16[2,64,256]{2,0,1:T(2,128)(2,1)} copy(bf16[2,64,256]{2,1,0:T(8,128)(2,1)S(1)} %bitcast.27) | data formatting | bytes 131072 | tf_op jit(solution)/shard_map/reshape | solution.py:385
  (1 shorter events, 0.0 us)
Async XLA Ops:
  6.9 1.0 %copy-start = (bf16[2,2048,64]{1,2,0:T(8,128)(2,1)S(1)}, bf16[2,2048,64]{1,2,0:T(8,128)(2,1)}, u32[]{:S(2)}) copy-start(bf16[2,2048,64]{1,2,0:T(8,128)(2,1)} %param.16) | copy-start | bytes 1572868
  7.9 0.9 %copy-start.1 = (bf16[2,16,16,256]{3,2,1,0:T(8,128)(2,1)S(1)}, bf16[2,16,16,256]{3,2,1,0:T(8,128)(2,1)}, u32[]{:S(2)}) copy-start(bf16[2,16,16,256]{3,2,1,0:T(8,128)(2,1)} %param.19) | copy-start | bytes 786436
  8.9 0.8 %copy-start.2 = (bf16[2,64,256]{2,1,0:T(8,128)(2,1)S(1)}, bf16[2,64,256]{2,1,0:T(8,128)(2,1)}, u32[]{:S(2)}) copy-start(bf16[2,64,256]{2,1,0:T(8,128)(2,1)} %up_hbm.1) | copy-start | bytes 196612
  9.7 0.8 %copy-start.3 = (s32[64,64]{1,0:T(8,128)S(1)}, s32[64,64]{1,0:T(8,128)}, u32[]{:S(2)}) copy-start(s32[64,64]{1,0:T(8,128)} %table_ref.1) | copy-start | bytes 49156

commit v3 on v2

--- a/solution.py
+++ b/solution.py
@@ -54,7 +54,7 @@
         sum_ref[:, h : h + 1] = jnp.where(here, total, sum_ref[:, h : h + 1])
 
 
-def add_fresh(q_ref, kn_ref, fresh, acc_ref, top_ref, sum_ref, out_ref, group):
+def fresh_scores(q_ref, kn_ref, first_ref, second_ref, group):
     tokens = q_ref.shape[0]
     rows = tokens // 2
     heads = q_ref.shape[1] // HEAD_WIDTH
@@ -64,34 +64,51 @@
         key_new = kn_ref[:, kv].astype(jnp.float32)
         k0 = jnp.concatenate([key_new[:rows], key_new[:rows]], axis=0)
         k1 = jnp.concatenate([key_new[rows:], key_new[rows:]], axis=0)
-        v_new = fresh[:, kv].astype(jnp.float32)
+        for h in range(k * group, (k + 1) * group):
+            q = q_ref[:, h * HEAD_WIDTH : (h + 1) * HEAD_WIDTH].astype(jnp.float32)
+            s0 = jnp.sum(q * k0, axis=1, keepdims=True) * scale
+            s1 = jnp.sum(q * k1, axis=1, keepdims=True) * scale
+            first_ref[:, h : h + 1] = s0
+            second_ref[:, h : h + 1] = jnp.where(second, s1, masked_score)
+
+
+def add_fresh(fresh, acc_ref, top_ref, sum_ref, first_ref, second_ref, out_ref, group):
+    rows = fresh.shape[0] // 2
+    heads = top_ref.shape[1]
+    s0, s1, top = first_ref[...], second_ref[...], top_ref[...]
+    largest = jnp.maximum(top, jnp.maximum(s0, s1))
+    keep = jnp.exp(top - largest)
+    e0 = jnp.exp(s0 - largest)
+    e1 = jnp.exp(s1 - largest)
+    share = 1.0 / (sum_ref[...] * keep + e0 + e1)
+    keep = keep * share
+    e0 = e0.astype(jnp.bfloat16).astype(jnp.float32) * share
+    e1 = e1.astype(jnp.bfloat16).astype(jnp.float32) * share
+    for k in range(heads // group):
+        v_new = fresh[:, k * HEAD_WIDTH : (k + 1) * HEAD_WIDTH].astype(jnp.float32)
         v0 = jnp.concatenate([v_new[:rows], v_new[:rows]], axis=0)
         v1 = jnp.concatenate([v_new[rows:], v_new[rows:]], axis=0)
         for h in range(k * group, (k + 1) * group):
             cols = slice(h * HEAD_WIDTH, (h + 1) * HEAD_WIDTH)
-            q = q_ref[:, cols].astype(jnp.float32)
-            s0 = jnp.sum(q * k0, axis=1, keepdims=True) * scale
-            s1 = jnp.sum(q * k1, axis=1, keepdims=True) * scale
-            s1 = jnp.where(second, s1, masked_score)
-            top = top_ref[:, h : h + 1]
-            largest = jnp.maximum(top, jnp.maximum(s0, s1))
-            keep = jnp.exp(top - largest)
-            e0 = jnp.exp(s0 - largest)
-            e1 = jnp.exp(s1 - largest)
-            total = sum_ref[:, h : h + 1] * keep + e0 + e1
-            mixed = acc_ref[:, cols] * keep
-            mixed = mixed + e0.astype(jnp.bfloat16).astype(jnp.float32) * v0
-            mixed = mixed + e1.astype(jnp.bfloat16).astype(jnp.float32) * v1
-            out_ref[:, cols] = (mixed / total).astype(jnp.bfloat16)
+            one = slice(h, h + 1)
+            mixed = acc_ref[:, cols] * keep[:, one] + e0[:, one] * v0 + e1[:, one] * v1
+            out_ref[:, cols] = mixed.astype(jnp.bfloat16)
+
+
+def as_column(row):
+    count = row.shape[1]
+    across = lax.broadcasted_iota(jnp.int32, (count, count), 1)
+    down = lax.broadcasted_iota(jnp.int32, (count, count), 0)
+    return jnp.sum(jnp.where(across == down, row, 0), axis=1, keepdims=True)
 
 
 def serving_kernel(
     stores, parts, pages, page_len, group,
-    x_ref, q_ref, kn_ref, table_ref, length_ref, holder_ref, named_ref,
+    x_ref, q_ref, kn_ref, table_ref, length_ref, named_ref, listed_ref, dest_ref,
     value_hbm, down_hbm, up_hbm, pool_hbm,
     out_ref, fresh_ref,
     value_ref, down_ref, up_ref, pool_ref, base_send, base_recv, mid_send, mid_recv,
-    acc_ref, top_ref, sum_ref, count_ref,
+    acc_ref, top_ref, sum_ref, count_ref, first_ref, second_ref, holder_ref,
     local_sem, line_send, line_recv, pair_send, pair_recv, base_ssem, base_rsem,
     mid_ssem, mid_rsem,
 ):
@@ -176,8 +193,7 @@
                     pair(stream, me + 1 + t, half).start()
 
     def attend(slot):
-        holder = jnp.concatenate([holder_ref[...], holder_ref[...]], axis=0)
-        here = holder == slot
+        here = holder_ref[...] == slot
         pool_attention(
             q_ref, pool_ref[slot, 0], pool_ref[slot, 1], jnp.where(here, count_ref[...], 0.0),
             here, acc_ref, top_ref, sum_ref, group,
@@ -219,12 +235,19 @@
     for d in range(1, parts):
         base_copy(d).start()
 
-    counts = position_counts(table_ref[...], length_ref[...], pages, page_len)
+    rows = tokens // 2
+    hits = listed_ref[...] == lax.broadcasted_iota(
+        jnp.int32, (rows, listed_ref.shape[1]), 0
+    )
+    holder = me + jnp.sum(jnp.where(hits, dest_ref[...] - me, 0), axis=1, keepdims=True)
+    holder_ref[...] = jnp.concatenate([holder, holder], axis=0)
+    counts = position_counts(table_ref[...], as_column(length_ref[...]), pages, page_len)
     count_ref[...] = jnp.concatenate([counts, counts], axis=0)
     acc_ref[...] = jnp.zeros_like(acc_ref)
     top_ref[...] = jnp.zeros_like(top_ref)
     sum_ref[...] = jnp.zeros_like(sum_ref)
     attend(me)
+    fresh_scores(q_ref, kn_ref, first_ref, second_ref, group)
     arrivals(0, (0, 1), True)
     arrivals(0, (2,), False)
 
@@ -241,7 +264,8 @@
 
     lax.fori_loop(1, stores - 1, step, 0)
 
-    named = jnp.concatenate([named_ref[...], named_ref[...]], axis=0)
+    named = as_column(named_ref[...])
+    named = jnp.concatenate([named, named], axis=0)
     lane = lax.broadcasted_iota(jnp.int32, (tokens, resident), 1)
     own_lane = lane // (resident // 2)
 
@@ -283,7 +307,7 @@
     term = lax.fori_loop(0, stores, upward, jnp.zeros((tokens, width), jnp.float32))
     fresh = (base + adapter_scale * term).astype(jnp.bfloat16)
     fresh_ref[...] = fresh
-    add_fresh(q_ref, kn_ref, fresh, acc_ref, top_ref, sum_ref, out_ref, group)
+    add_fresh(fresh, acc_ref, top_ref, sum_ref, first_ref, second_ref, out_ref, group)
 
     def finish(t, carry):
         sends(t, lambda copy: copy.wait_send())
@@ -317,7 +341,6 @@
     relocated_destination,
 ):
     stores = lax.axis_size("store")
-    me = lax.axis_index("store")
     rows, steps, feats = hidden.shape
     tokens = rows * steps
     width = fresh_rotated_keys.shape[2]
@@ -335,10 +358,6 @@
     up = adapter_up_factors.reshape(2, resident // 2, width)
     pool = key_value_pool.reshape(2, span, width)
 
-    hits = relocated_rows[None, :] == jnp.arange(rows, dtype=jnp.int32)[:, None]
-    away = jnp.sum(jnp.where(hits, relocated_destination[:, 0][None, :] - me, 0), axis=1)
-    holder = (me + away)[:, None]
-
     heads = q_width // HEAD_WIDTH
     dma = pltpu.SemaphoreType.DMA
     attention, fresh = pl.pallas_call(
@@ -347,8 +366,8 @@
             jax.ShapeDtypeStruct((tokens, q_width), jnp.bfloat16),
             jax.ShapeDtypeStruct((tokens, width), jnp.bfloat16),
         ),
-        in_specs=[pl.BlockSpec(memory_space=pltpu.VMEM)] * 7
-        + [pl.BlockSpec(memory_space=pl.ANY)] * 4,
+        in_specs=[pl.BlockSpec(memory_space=pltpu.VMEM)] * 8
+        + [pl.BlockSpec(memory_space=pltpu.HBM)] * 4,
         out_specs=[pl.BlockSpec(memory_space=pltpu.VMEM)] * 2,
         scratch_shapes=[
             pltpu.VMEM(value_matrix.shape, jnp.bfloat16),
@@ -363,6 +382,9 @@
             pltpu.VMEM((tokens, heads), jnp.float32),
             pltpu.VMEM((tokens, heads), jnp.float32),
             pltpu.VMEM((tokens, span), jnp.float32),
+            pltpu.VMEM((tokens, heads), jnp.float32),
+            pltpu.VMEM((tokens, heads), jnp.float32),
+            pltpu.VMEM((tokens, 1), jnp.int32),
             dma((4,)),
             dma((3, 2, stores)),
             dma((3, stores)),
@@ -374,10 +396,12 @@
             dma((parts - 1,)),
         ],
         compiler_params=pltpu.CompilerParams(
-            collective_id=0, has_side_effects=True, vmem_limit_bytes=48 * 1024 * 1024
+            collective_id=0, has_side_effects=True, vmem_limit_bytes=62 * 1024 * 1024
         ),
     )(
-        x, q, kn, row_page_table, context_length[:, None], holder, adapter_index_rows,
+        x, q, kn, row_page_table, context_length[None, :],
+        adapter_index_rows.reshape(1, rows), relocated_rows[None, :],
+        relocated_destination.reshape(1, relocated_rows.shape[0]),
         value_matrix, down, up, pool,
     )
     return (

time: 70.1 us -> 67.4 us (0.961)
  other arithmetic: 1.41 us -> 0 us
  local copies, waits for them, and re-layouts: 10.4 us -> 9.37 us
    unnamed x9 -> x0, local copies, waits for them, and re-layouts: 4.33 us -> none
    reshape x1, local copies, waits for them, and re-layouts: 1.33 us -> 2.37 us  [per_device(): attention.reshape(steps, rows, q_width).transpose(1, 0, 2)]
    reshape x1, local copies, waits for them, and re-layouts: 0.7 us -> 1.54 us  [per_device(): fresh.reshape(steps, rows, width).transpose(1, 0, 2)]
    transpose x1, local copies, waits for them, and re-layouts: 1.2 us -> 1.99 us  [per_device(): x = hidden.transpose(1, 0, 2).reshape(tokens, feats)]
    transpose x1, local copies, waits for them, and re-layouts: 1.2 us -> 1.98 us  [per_device(): q = queries.transpose(1, 0, 2).reshape(tokens, q_width)]
    broadcast_in_dim x1 -> x0, local copies, waits for them, and re-layouts: 0.74 us -> none  [per_device(): context_length[:, None]]
    reduce_sum x1 -> x0, other arithmetic: 0.74 us -> none  [per_device(): jnp.sum(jnp.where(hits, relocated_destination[:, 0][None, :] - me, 0), ax...]
where the time goes in v3:
time: 67.4 us; the launch traced here: 67 us
  Pallas kernels  57 us (85%)
  local copies, waits for them, and re-layouts  9.37 us (14%)
    pallas_call x1, Pallas kernels, per_device(): pl.pallas_call(functools.partial(serving_kernel, stores, parts, pages, pa...  57 us
    reshape x1, local copies, waits for them, and re-layouts, per_device(): attention.reshape(steps, rows, q_width).transpose(1, 0, 2)  2.37 us
    transpose x1, local copies, waits for them, and re-layouts, per_device(): x = hidden.transpose(1, 0, 2).reshape(tokens, feats)  1.99 us
    transpose x1, local copies, waits for them, and re-layouts, per_device(): q = queries.transpose(1, 0, 2).reshape(tokens, q_width)  1.98 us
    reshape x1, local copies, waits for them, and re-layouts, per_device(): fresh.reshape(steps, rows, width).transpose(1, 0, 2)  1.54 us
    transpose x1, local copies, waits for them, and re-layouts, per_device(): kn = fresh_rotated_keys.transpose(1, 0, 2).reshape(tokens, width)  1.48 us

profile of v3, /device:TPU:0, one launch (start us, length us, event | category | flops | bytes accessed | tf_op | source)
XLA Modules:
  0.0 67.0 jit_solution(10081085680859099790)
XLA Ops:
  0.6 1.5 %copy.16 = bf16[2,64,256]{2,1,0:T(8,128)(2,1)} copy(bf16[2,64,256]{2,0,1:T(2,128)(2,1)} %bitcast.29) | data formatting | bytes 131072 | tf_op jit(solution)/shard_map/transpose | solution.py:356
  2.1 2.0 %copy.14 = bf16[2,64,2048]{2,1,0:T(8,128)(2,1)} copy(bf16[2,64,2048]{2,0,1:T(2,128)(2,1)} %bitcast.22) | data formatting | bytes 1048576 | tf_op jit(solution)/shard_map/transpose | solution.py:354
  4.1 2.0 %copy.15 = bf16[2,64,2048]{2,1,0:T(8,128)(2,1)} copy(bf16[2,64,2048]{2,0,1:T(2,128)(2,1)} %bitcast.23) | data formatting | bytes 1048576 | tf_op jit(solution)/shard_map/transpose | solution.py:355
  6.1 57.0 %shard_map.131 = (bf16[128,2048]{1,0:T(8,128)(2,1)}, bf16[128,256]{1,0:T(8,128)(2,1)}) custom-call(bf16[128,2048]{1,0:T(8,128)(2,1)} %bitcast.20, bf16[128,2048]{1,0:T(8,128)(2,1)} %bitcast.21, bf16[128,256]{1,0:T(8,128)(2,1)} %bitcast.27, s32[64,64]{1,0:T(8,128)} %table_ref.1, s32[1,64]{1,0:T(1,128)} %bitcast.32, s32[1,64]{1,0:T(1,128)} %bitcast.33, ...), custom_call_target="tpu_custom_call" | custom-call | tf_op jit(solution)/shard_map/pallas_call | solution.py:363
  63.1 2.4 %copy.21 = bf16[2,64,2048]{2,0,1:T(2,128)(2,1)} copy(bf16[2,64,2048]{2,1,0:T(8,128)(2,1)} %bitcast.25) | data formatting | bytes 1048576 | tf_op jit(solution)/shard_map/reshape | solution.py:408
  65.5 1.5 %copy.22 = bf16[2,64,256]{2,0,1:T(2,128)(2,1)} copy(bf16[2,64,256]{2,1,0:T(8,128)(2,1)} %bitcast.31) | data formatting | bytes 131072 | tf_op jit(solution)/shard_map/reshape | solution.py:409
